TPU v7x, 256 devices: a whole 4x4x8 slice. The times are simulated.
256 devices in a mesh: dp: 16 (over y_lo, z), ctx: 16 (over x, y_hi, core).
Axes of the slice: x: 4, y: 4 (y_hi: 2, y_lo: 2; y = y_hi * 2 + y_lo), z: 8, core: 2. Of those that a mesh axis runs over, the one named last changes fastest.
Arguments:
- queries: bfloat16 [16, 2048, 4096], P('dp', 'ctx'), may hold values from -9 to 9
- keys: bfloat16 [16, 2048, 512], P('dp', 'ctx'), may hold values from -7 to 7
- values: bfloat16 [16, 2048, 512], P('dp', 'ctx'), may hold values from -6 to 6
- cotangent: bfloat16 [16, 2048, 4096], P('dp', 'ctx'), may hold values from -6 to 6
- live: int32 [16, 2048], P('dp', 'ctx'), may hold values from 0 to 1, as said below
- docs: int32 [16, 2048], P('dp'), may hold values from 0 to 5, never falling along the last dimension, each value on 1 to 1024 neighbouring positions
Outputs:
- attended: bfloat16 [16, 2048, 4096], P('dp', 'ctx')
- grad_queries: bfloat16 [16, 2048, 4096], P('dp', 'ctx')
- key_gradient: bfloat16 [16, 2048, 512], P('dp', 'ctx')
- value_gradient: bfloat16 [16, 2048, 512], P('dp', 'ctx')
Inputs may be any that keep to these rules, and one draw needn't show every extreme that they name: `docs`: never falls along a sequence; each document spans 1 to 1024 positions and one spans exactly 1024. `live`: row 0 of every sequence is 1.
All inputs are finite; a program needn't handle non-finite values.
Results may differ from a plain program's by a relative error of at most 0.02.
Values may be sent and summed in bfloat16 or wider, within the bound.
No kernel may reach another device: no remote copies, remote signals or barrier semaphores. Data moves between devices by JAX's collectives and lax.ppermute only.
A program may use at most 64 MiB of HBM per device.

v0:
```python
from functools import partial
import math

import jax
import jax.numpy as jnp
from jax import lax
from jax.sharding import PartitionSpec as P

HEAD_SIZE = 128


masked_fill = -1e30


def shard_positions(shard_index, devices, shard_rows):
    half_rows = shard_rows // 2
    offsets = jnp.arange(shard_rows, dtype=jnp.int32)
    piece_id = jnp.where(offsets < half_rows, shard_index, 2 * devices - 1 - shard_index)
    return piece_id * half_rows + offsets % half_rows


def shard_documents(doc_table, shard_index, devices):
    first_half = lax.dynamic_index_in_dim(doc_table, shard_index, 0, keepdims=False)
    second_half = lax.dynamic_index_in_dim(
        doc_table, 2 * devices - 1 - shard_index, 0, keepdims=False
    )
    return jnp.concatenate([first_half, second_half])


def widen(source, low, high, length, axis_pos, filler):
    padding = [(0, 0)] * source.ndim
    padding[axis_pos] = (low, length - high)
    return jnp.pad(source, padding, constant_values=filler)


def on_device(queries, keys, values, cotangent, live, docs):
    devices = lax.axis_size("ctx")
    ctx_index = lax.axis_index("ctx")
    shard_rows = queries.shape[1]
    half_rows = shard_rows // 2
    kv_width = keys.shape[2]
    kv_heads = kv_width // HEAD_SIZE
    query_group_width = queries.shape[2] // kv_width
    score_scale = 1.0 / math.sqrt(HEAD_SIZE)
    live_count = lax.psum(jnp.sum(live), ("dp", "ctx"))
    loss_ratio = lax.axis_size("dp") * devices * shard_rows / live_count.astype(jnp.float32)
    doc_table = docs[0].reshape(2 * devices, half_rows)
    query_pos = shard_positions(ctx_index, devices, shard_rows)
    query_doc = shard_documents(doc_table, ctx_index, devices)
    query_fourfold = queries[0].reshape(shard_rows, kv_heads, query_group_width, HEAD_SIZE)
    full_keys, full_values = (
        lax.all_gather(keys[0], "ctx", axis=0, tiled=True),
        lax.all_gather(values[0], "ctx", axis=0, tiled=True),
    )

    def key_shard(shard_id):
        row_start = shard_id * shard_rows
        key_tile = lax.dynamic_slice_in_dim(full_keys, row_start, shard_rows, 0).reshape(
            shard_rows, kv_heads, HEAD_SIZE
        )
        value_tile = lax.dynamic_slice_in_dim(full_values, row_start, shard_rows, 0).reshape(
            shard_rows, kv_heads, HEAD_SIZE
        )
        key_pos = shard_positions(shard_id, devices, shard_rows)
        key_doc = shard_documents(doc_table, shard_id, devices)
        zig_case = jnp.where(shard_id < ctx_index, 0, jnp.where(shard_id > ctx_index, 2, 1))
        return (key_tile, value_tile, key_pos, key_doc, zig_case)

    def folded_case(zig_case, tile_fn):
        return lax.switch(
            zig_case,
            [
                partial(tile_fn, 0, shard_rows, 0, half_rows),
                partial(tile_fn, 0, shard_rows, 0, shard_rows),
                partial(tile_fn, half_rows, shard_rows, 0, shard_rows),
            ],
        )

    def pair_mask(key_pos, key_doc, query_low, query_high, key_low, key_high):
        return (query_doc[query_low:query_high, None] == key_doc[None, key_low:key_high]) & (
            key_pos[None, key_low:key_high] <= query_pos[query_low:query_high, None]
        )

    def tile_scores(key_tile, query_low, query_high, key_low, key_high):
        return (
            jnp.einsum(
                "qgjd,kgd->gjqk",
                query_fourfold[query_low:query_high],
                key_tile[key_low:key_high],
                preferred_element_type=jnp.float32,
            )
            * score_scale
        )

    def stats_tile(key_tile, key_pos, key_doc, query_low, query_high, key_low, key_high):
        allowed = pair_mask(key_pos, key_doc, query_low, query_high, key_low, key_high)
        masked = jnp.where(
            allowed, tile_scores(key_tile, query_low, query_high, key_low, key_high), masked_fill
        )
        row_peak = jnp.max(masked, axis=-1)
        row_mass = jnp.sum(jnp.where(allowed, jnp.exp(masked - row_peak[..., None]), 0.0), axis=-1)
        row_peak, row_mass = (row_peak, row_mass)
        return (
            widen(row_peak, query_low, query_high, shard_rows, 2, masked_fill),
            widen(row_mass, query_low, query_high, shard_rows, 2, 0.0),
        )

    def stats_step(shard_id, state_now):
        run_peak, run_mass = state_now
        key_tile, value_tile, key_pos, key_doc, zig_case = key_shard(shard_id)
        tile_peak, tile_mass = folded_case(
            zig_case, partial(stats_tile, key_tile, key_pos, key_doc)
        )
        merged = jnp.maximum(run_peak, tile_peak)
        return (
            merged,
            run_mass * jnp.exp(run_peak - merged) + tile_mass * jnp.exp(tile_peak - merged),
        )

    stat_shape = (kv_heads, query_group_width, shard_rows)
    run_peak, run_mass = lax.fori_loop(
        0,
        devices,
        stats_step,
        (jnp.full(stat_shape, masked_fill, jnp.float32), jnp.zeros(stat_shape, jnp.float32)),
    )
    log_total = run_peak + jnp.log(run_mass)

    def tile_weights(key_tile, allowed, query_low, query_high, key_low, key_high):
        masked = jnp.where(
            allowed, tile_scores(key_tile, query_low, query_high, key_low, key_high), masked_fill
        )
        return jnp.where(
            allowed, jnp.exp(masked - log_total[:, :, query_low:query_high, None]), 0.0
        )

    def output_tile(
        key_tile, value_tile, key_pos, key_doc, query_low, query_high, key_low, key_high
    ):
        allowed = pair_mask(key_pos, key_doc, query_low, query_high, key_low, key_high)
        rounded = tile_weights(key_tile, allowed, query_low, query_high, key_low, key_high).astype(
            jnp.bfloat16
        )
        return widen(
            jnp.einsum(
                "gjqk,kgd->qgjd",
                rounded,
                value_tile[key_low:key_high],
                preferred_element_type=jnp.float32,
            ),
            query_low,
            query_high,
            shard_rows,
            0,
            0.0,
        )

    def output_step(shard_id, running):
        key_tile, value_tile, key_pos, key_doc, zig_case = key_shard(shard_id)
        return running + folded_case(
            zig_case, partial(output_tile, key_tile, value_tile, key_pos, key_doc)
        )

    row_shape = (shard_rows, kv_heads, query_group_width, HEAD_SIZE)
    attended = lax.fori_loop(0, devices, output_step, jnp.zeros(row_shape, jnp.float32)).astype(
        jnp.bfloat16
    )
    output_gradient = (
        cotangent[0].astype(jnp.float32) * live[0].astype(jnp.float32)[:, None] * loss_ratio
    ).astype(jnp.bfloat16)
    gradient_fourfold = output_gradient.reshape(row_shape)
    delta = jnp.transpose(
        jnp.sum(gradient_fourfold.astype(jnp.float32) * attended.astype(jnp.float32), axis=-1),
        (1, 2, 0),
    )

    def grad_tile(key_tile, value_tile, key_pos, key_doc, query_low, query_high, key_low, key_high):
        allowed = pair_mask(key_pos, key_doc, query_low, query_high, key_low, key_high)
        query_part = query_fourfold[query_low:query_high]
        grad_part = gradient_fourfold[query_low:query_high]
        weights = tile_weights(key_tile, allowed, query_low, query_high, key_low, key_high)
        rounded = weights.astype(jnp.bfloat16)
        pushes = jnp.einsum(
            "qgjd,kgd->gjqk",
            grad_part,
            value_tile[key_low:key_high],
            preferred_element_type=jnp.float32,
        )
        slopes = (
            weights * (pushes - delta[:, :, query_low:query_high, None]) * score_scale
        ).astype(jnp.bfloat16)
        grad_rows = jnp.einsum(
            "gjqk,kgd->qgjd", slopes, key_tile[key_low:key_high], preferred_element_type=jnp.float32
        )
        key_part = jnp.einsum(
            "gjqk,qgjd->kgd", slopes, query_part, preferred_element_type=jnp.float32
        )
        value_part = jnp.einsum(
            "gjqk,qgjd->kgd", rounded, grad_part, preferred_element_type=jnp.float32
        )
        grad_rows, key_part, value_part = (grad_rows, key_part, value_part)
        key_part = lax.optimization_barrier(key_part.astype(jnp.bfloat16)).astype(jnp.float32)
        value_part = lax.optimization_barrier(value_part.astype(jnp.bfloat16)).astype(jnp.float32)
        return (
            widen(grad_rows, query_low, query_high, shard_rows, 0, 0.0),
            widen(key_part, key_low, key_high, shard_rows, 0, 0.0).reshape(shard_rows, kv_width),
            widen(value_part, key_low, key_high, shard_rows, 0, 0.0).reshape(shard_rows, kv_width),
        )

    def scatter_step(shard_id, state_now):
        query_total, key_terms, value_terms = state_now
        key_tile, value_tile, key_pos, key_doc, zig_case = key_shard(shard_id)
        grad_rows, key_part, value_part = folded_case(
            zig_case, partial(grad_tile, key_tile, value_tile, key_pos, key_doc)
        )
        key_terms = lax.dynamic_update_slice_in_dim(
            key_terms, key_part.astype(jnp.bfloat16), shard_id * shard_rows, 0
        )
        value_terms = lax.dynamic_update_slice_in_dim(
            value_terms, value_part.astype(jnp.bfloat16), shard_id * shard_rows, 0
        )
        return (query_total + grad_rows, key_terms, value_terms)

    term_shape = (devices * shard_rows, kv_width)
    query_total, key_terms, value_terms = lax.fori_loop(
        0,
        devices,
        scatter_step,
        (
            jnp.zeros(row_shape, jnp.float32),
            jnp.zeros(term_shape, jnp.bfloat16),
            jnp.zeros(term_shape, jnp.bfloat16),
        ),
    )
    key_sums, value_sums = (
        lax.psum_scatter(
            key_terms.astype(jnp.float32).astype(jnp.bfloat16),
            "ctx",
            scatter_dimension=0,
            tiled=True,
        ).astype(jnp.float32),
        lax.psum_scatter(
            value_terms.astype(jnp.float32).astype(jnp.bfloat16),
            "ctx",
            scatter_dimension=0,
            tiled=True,
        ).astype(jnp.float32),
    )
    attended_out = attended.reshape(shard_rows, kv_width * query_group_width)[None]
    grad_queries = query_total.astype(jnp.bfloat16).reshape(
        shard_rows, kv_width * query_group_width
    )[None]
    key_gradient = key_sums.astype(jnp.bfloat16)[None]
    value_gradient = value_sums.astype(jnp.bfloat16)[None]
    return (attended_out, grad_queries, key_gradient, value_gradient)


def solution(mesh):
    in_specs = (
        P("dp", "ctx", None),
        P("dp", "ctx", None),
        P("dp", "ctx", None),
        P("dp", "ctx", None),
        P("dp", "ctx"),
        P("dp", None),
    )
    out_specs = (
        P("dp", "ctx", None),
        P("dp", "ctx", None),
        P("dp", "ctx", None),
        P("dp", "ctx", None),
    )
    return jax.shard_map(
        on_device, mesh=mesh, in_specs=in_specs, out_specs=out_specs, check_vma=False
    )
```

profile of v0, /device:TPU:31, one launch (start us, length us, event | category | flops | bytes accessed | tf_op | source)
XLA Modules:
  0.0 780.7 jit_solution(8076185474818151786)
XLA Ops:
  17.7 77.1 %psum.7 = s32[]{:T(128)} all-reduce(s32[]{:T(128)} %get-tuple-element.1678), channel_id=1, replica_groups=mesh['dp'=16,'ctx'=16] {'dp','ctx'}, use_global_device_ids=true, to_apply=%region_17.18 | all-reduce | flops 1 | bytes 8 | tf_op jit(solution)/shard_map/psum | solution.py:45
  99.5 87.1 %while.60 = (s32[]{:T(128)}, f32[4,8,128]{2,1,0:T(8,128)S(1)}, f32[4,8,128]{2,1,0:T(8,128)S(1)}, s32[]{:T(128)}, s32[32,64]{1,0:T(8,128)}, /*index=5*/bf16[2048,...) while((s32[]{:T(128)}, f32[4,8,128]{2,1,0:T(8,128)S(1)}, ...), condition=%wide.region_10.11_spmd.clone.clone.clone, body=%wide.region_0.10_spmd.clone.clone.clone.sunk | while | flops 138487568 | bytes 5838339 | solution.py:121
  186.6 149.4 %while.61 = (s32[]{:T(128)}, f32[128,4,8,128]{3,0,2,1:T(8,128)}, s32[]{:T(128)}, s32[32,64]{1,0:T(8,128)}, bf16[2048,512]{0,1:T(8,128)(2,1)}, /*index=5*/bf16[20...) while((s32[]{:T(128)}, f32[128,4,8,128]{3,0,2,1:T(8,128)}, ...), condition=%wide.region_15.16_spmd.clone.clone.clone, body=%wide.region_11.15_spmd.clone.clone.clone.sunk | while | flops 272156416 | bytes 13157999 | solution.py:165
  344.1 232.2 %while.62 = (s32[]{:T(128)}, f32[128,4,8,128]{3,0,2,1:T(8,128)}, bf16[2048,512]{1,0:T(8,128)(2,1)}, bf16[2048,512]{1,0:T(8,128)(2,1)}, s32[]{:T(128)}, /*index=5...) while((s32[]{:T(128)}, f32[128,4,8,128]{3,0,2,1:T(8,128)}, ...), condition=%wide.region_23.24_spmd.clone.clone.clone, body=%wide.region_19.23_spmd.clone.clone.clone.sunk | while | flops 677038720 | bytes 33236716 | solution.py:225
  347.4 6.2 conditional.26
  361.1 6.2 conditional.26
  367.3 4.0 select_add_fusion.5
  375.5 6.2 conditional.26
  381.7 4.0 select_add_fusion.5
  389.9 6.2 conditional.26
  396.1 4.0 select_add_fusion.5
  404.3 6.2 conditional.26
  410.5 4.0 select_add_fusion.5
  418.7 6.2 conditional.26
  424.9 4.0 select_add_fusion.5
  433.1 6.2 conditional.26
  439.3 4.0 select_add_fusion.5
  447.5 6.2 conditional.26
  453.7 4.0 select_add_fusion.5
  461.9 6.2 conditional.26
  476.3 6.2 conditional.26
  490.7 6.2 conditional.26
  505.1 6.2 conditional.26
  519.4 6.2 conditional.26
  525.7 4.0 select_add_fusion.5
  533.9 6.2 conditional.26
  540.1 4.0 select_add_fusion.5
  548.3 6.2 conditional.26
  562.7 8.7 %conditional.26 = (f32[128,4,8,128]{3,0,2,1:T(8,128)}, bf16[128,512]{0,1:T(8,128)(2,1)S(1)}, bf16[128,512]{0,1:T(8,128)(2,1)S(1)}) conditional(s32[]{:T(128)} %clamp.44, (s32[128]{0:T(128)}, s32[64]{0:T(128)S(1)}, s32[128]{0:T(128)S(1)}, s32[128]{0:T(128)S(1)}, bf16[128,4,128]{0,2,1:T(8,128)(2,1)S(1)}, ...), branch_computations={%region_20.20_spmd, %region_21.21_spmd, %region_22.22_spmd} | conditional | flops 675987456 | bytes 25368684
  571.4 4.0 select_add_fusion.5
  581.0 110.7 %reduce-scatter.3.cloned.1.call-done = bf16[128,512]{1,0:T(8,128)(2,1)} async-done(((bf16[2048,512]{1,0:T(8,128)(2,1)}), bf16[128,512]{1,0:T(8,128)(2,1)}) %reduce-scatter.3.cloned.1.call-update) | async-done | bytes 131088 | tf_op jit(solution)/shard_map/reduce_scatter | solution.py:236
  691.7 82.4 %reduce-scatter.5.cloned.1.call-done = bf16[128,512]{1,0:T(8,128)(2,1)} async-done(((bf16[2048,512]{1,0:T(8,128)(2,1)}), bf16[128,512]{1,0:T(8,128)(2,1)}) %reduce-scatter.5.cloned.1.call-update) | async-done | bytes 131088 | tf_op jit(solution)/shard_map/reduce_scatter | solution.py:242
  (735 shorter events, 558.5 us)
Async XLA Ops:
  7.2 92.3 %all-gather.5.cloned.1.call-start = ((), (), s32[]{:S(2)}) async-start(), calls=%async_computation.4 | async-start | bytes 2228224 | tf_op jit(solution)/shard_map/all_gather | solution.py:52
  8.9 177.7 %all-gather.7.cloned.1.call-start = ((), (), s32[]{:S(2)}) async-start(), calls=%async_computation.5 | async-start | bytes 2228224 | tf_op jit(solution)/shard_map/all_gather | solution.py:53
  10.6 681.1 %reduce-scatter.3.cloned.1.call-start = ((), (), s32[]{:S(2)}) async-start(), calls=%async_computation.2 | async-start | bytes 2228224 | tf_op jit(solution)/shard_map/reduce_scatter | solution.py:236
  12.3 2.9 copy-start.15
  12.4 4.2 copy-start.17
  12.4 83.2 %copy-start.6 = (bf16[1,128,4096]{2,1,0:T(8,128)(2,1)S(1)}, bf16[1,128,4096]{2,1,0:T(8,128)(2,1)}, u32[]{:S(2)}) copy-start(bf16[1,128,4096]{2,1,0:T(8,128)(2,1)} %param.24) | copy-start | bytes 3145732
  329.0 0.5 copy-start.7
  329.0 0.5 copy-start.11
  336.0 1.9 copy-start.4
  336.0 2.0 copy-start.5
  336.0 2.0 copy-start.16
  338.0 1.5 copy-start.2
  562.7 0.5 copy-start.9
  562.7 0.5 copy-start.13
  565.4 1.3 copy-start
  576.3 1.2 copy-start.3
  576.4 197.8 %reduce-scatter.5.cloned.1.call-start = ((), (), s32[]{:S(2)}) async-start(), calls=%async_computation.3 | async-start | bytes 2228224 | tf_op jit(solution)/shard_map/reduce_scatter | solution.py:242
  576.4 2.5 copy-start.1
Sparse Core Ops, SparseCore 0:
  11.1 55.8 all-gather.4
  70.1 53.6 all-gather.6
  576.5 115.1 reduce-scatter.2
  696.4 77.7 reduce-scatter.4
where the time goes:
time: 794 us; the launch traced here: 781 us
  other arithmetic  222 us (28%)
  waiting for transfers between devices  194 us (24%)
  local copies, waits for them, and re-layouts  147 us (19%)
  matrix products  122 us (15%)
  blocking collectives  77.1 us (10%)
  between operations  14.7 us (2%)
    reduce_scatter x1, waiting for transfers between devices, on_device(): lax.psum_scatter(key_terms.astype(jnp.float32).astype(jnp.bfloat16), 'ctx...  111 us
    reduce_scatter x1, waiting for transfers between devices, on_device(): lax.psum_scatter(value_terms.astype(jnp.float32).astype(jnp.bfloat16), 'c...  82.4 us
    psum x1, blocking collectives, on_device(): live_count = lax.psum(jnp.sum(live), ('dp', 'ctx'))  77.1 us
    add x16, other arithmetic, scatter_step(): return (query_total + grad_rows, key_terms, value_terms)  62.9 us
    and x48, other arithmetic, pair_mask(): (query_doc[query_low:query_high, None] == key_doc[None, key_low:key_high]...  54.7 us
    add x16, other arithmetic, output_step(): running + folded_case(zig_case, partial(output_tile, key_tile, value_tile...  50.8 us
    dot_general x32, matrix products, tile_scores(): jnp.einsum('qgjd,kgd->gjqk', query_fourfold[query_low:query_high], key_ti...  37.4 us
    dot_general x16, matrix products, output_tile(): jnp.einsum('gjqk,kgd->qgjd', rounded, value_tile[key_low:key_high], prefe...  34.5 us
  transfers between devices with their start and end apart: 4, of which 2 were waited for; matrix products, arithmetic and copies ran while one was open for 13% of the time, Pallas kernels for 0%

commit v1 on v0

v1 whole, which is shorter than its diff:
```python
from functools import partial
import math

import jax
import jax.numpy as jnp
from jax import lax
from jax.experimental import pallas as pl
from jax.experimental.pallas import tpu as pltpu
from jax.sharding import PartitionSpec as P

HEAD = 128
BLOCK = 128
TILE = 256
GROUPS = 2
FOLD = 8
ROWS = FOLD * BLOCK
MASKED = -1e30
SCALE = 1.0 / math.sqrt(HEAD)
SCALE_LOG2E = SCALE * math.log2(math.e)

NT = (((1,), (1,)), ((), ()))
NN = (((1,), (0,)), ((), ()))


def dot(a, b, dims=NN):
    return lax.dot_general(a, b, dims, preferred_element_type=jnp.float32)


def attention_kernel(
    info_ref,
    bounds_ref,
    q_own,
    q_sib,
    c_own,
    c_sib,
    *refs,
):
    chips = 8
    chunks = refs[:chips]
    o_own, o_sib, dq_own, dq_sib = refs[chips : chips + 4]
    terms = refs[chips + 4 : 2 * chips + 4]
    (
        k_nat,
        v_nat,
        s_ref,
        p_ref,
        q_ref,
        do_ref,
        qt_ref,
        dot_ref,
        m_ref,
        l_ref,
        o_ref,
        dq_ref,
        dkt_ref,
        dvt_ref,
    ) = refs[2 * chips + 4 :]

    for group in range(GROUPS):
        k_nat[group, 0:BLOCK, :] = jnp.zeros((BLOCK, HEAD), jnp.bfloat16)
        v_nat[group, 0:BLOCK, :] = jnp.zeros((BLOCK, HEAD), jnp.bfloat16)
    for at, chunk in enumerate(chunks):
        low = info_ref[4 + at]
        for half in range(2):
            block = low if half == 0 else 15 - low
            place = pl.ds(pl.multiple_of((block + 1) * BLOCK, BLOCK), BLOCK)
            rows = slice(half * BLOCK, (half + 1) * BLOCK)
            for group in range(GROUPS):
                k_nat[group, place, :] = chunk[rows, group * HEAD : (group + 1) * HEAD]
                v_nat[group, place, :] = chunk[
                    rows, (GROUPS + group) * HEAD : (GROUPS + group + 1) * HEAD
                ]

    for group in range(GROUPS):
        dkt_ref[...] = jnp.zeros_like(dkt_ref)
        dvt_ref[...] = jnp.zeros_like(dvt_ref)
        for half in range(2):
            tiles = info_ref[half]
            end = info_ref[2 + half]
            rows = slice(half * 64, half * 64 + 64)
            low_bound = bounds_ref[half * BLOCK : (half + 1) * BLOCK, 0:1]
            own_pos = bounds_ref[half * BLOCK : (half + 1) * BLOCK, 1:2]
            live = bounds_ref[half * BLOCK : (half + 1) * BLOCK, 2:3].astype(jnp.float32)

            def columns(head):
                return slice((group * FOLD + head) * HEAD, (group * FOLD + head + 1) * HEAD)

            for head in range(FOLD):
                q_ref[head * BLOCK : head * BLOCK + 64, :] = q_own[rows, columns(head)]
                q_ref[head * BLOCK + 64 : (head + 1) * BLOCK, :] = q_sib[rows, columns(head)]
            m_ref[...] = jnp.full_like(m_ref, MASKED)
            l_ref[...] = jnp.zeros_like(l_ref)
            o_ref[...] = jnp.zeros_like(o_ref)
            dq_ref[...] = jnp.zeros_like(dq_ref)

            def key_rows(j):
                return pl.ds(pl.multiple_of(end - TILE * (j + 1) + BLOCK, BLOCK), TILE)

            def tile_columns(j):
                return pl.ds(pl.multiple_of(j * TILE, TILE), TILE)

            def score_tile(j, _):
                first = end - TILE * (j + 1)
                key_pos = first + lax.broadcasted_iota(jnp.int32, (BLOCK, TILE), 1)
                bias = jnp.where((key_pos >= low_bound) & (key_pos <= own_pos), 0.0, MASKED)
                scores = dot(q_ref[...], k_nat[group, key_rows(j), :], NT)
                scores = (
                    scores.reshape(FOLD, BLOCK, TILE) * SCALE_LOG2E + bias[None]
                ).reshape(ROWS, TILE)
                s_ref[:, tile_columns(j)] = scores
                m_ref[...] = jnp.maximum(
                    m_ref[...], jnp.maximum(scores[:, :HEAD], scores[:, HEAD:])
                )
                return 0

            lax.fori_loop(0, tiles, score_tile, 0)
            m_ref[...] = jnp.broadcast_to(
                jnp.max(m_ref[...], axis=1, keepdims=True), (ROWS, HEAD)
            )

            def weight_tile(j, _):
                peak = m_ref[...]
                scores = s_ref[:, tile_columns(j)]
                left = jnp.exp2(scores[:, :HEAD] - peak)
                right = jnp.exp2(scores[:, HEAD:] - peak)
                l_ref[...] += left + right
                weights = jnp.concatenate([left, right], axis=1).astype(jnp.bfloat16)
                p_ref[:, tile_columns(j)] = weights
                o_ref[...] += dot(weights, v_nat[group, key_rows(j), :])
                return 0

            lax.fori_loop(0, tiles, weight_tile, 0)
            for head in range(FOLD):
                span = slice(head * BLOCK, (head + 1) * BLOCK)
                inverse = 1.0 / jnp.sum(l_ref[span, :], axis=1, keepdims=True)
                out = (o_ref[span, :] * inverse).astype(jnp.bfloat16)
                o_own[rows, columns(head)] = out[:64]
                o_sib[rows, columns(head)] = out[64:]
                cot = jnp.concatenate(
                    [c_own[rows, columns(head)], c_sib[rows, columns(head)]], axis=0
                )
                grad = (cot.astype(jnp.float32) * (live * inverse)).astype(jnp.bfloat16)
                do_ref[span, :] = grad
                m_ref[span, :] = jnp.broadcast_to(
                    jnp.sum(
                        grad.astype(jnp.float32) * out.astype(jnp.float32), axis=1, keepdims=True
                    ),
                    (BLOCK, HEAD),
                )
            qt_ref[...] = q_ref[...].T
            dot_ref[...] = do_ref[...].T

            def gradient_tile(j, _):
                delta = m_ref[...]
                pushes = dot(do_ref[...], v_nat[group, key_rows(j), :], NT)
                weights = p_ref[:, tile_columns(j)]
                wide = weights.astype(jnp.float32)
                slopes = jnp.concatenate(
                    [
                        wide[:, :HEAD] * (pushes[:, :HEAD] - delta),
                        wide[:, HEAD:] * (pushes[:, HEAD:] - delta),
                    ],
                    axis=1,
                ).astype(jnp.bfloat16)
                dq_ref[...] += dot(slopes, k_nat[group, key_rows(j), :])
                dkt_ref[:, key_rows(j)] += dot(qt_ref[...], slopes)
                dvt_ref[:, key_rows(j)] += dot(dot_ref[...], weights)
                return 0

            lax.fori_loop(0, tiles, gradient_tile, 0)
            for head in range(FOLD):
                span = slice(head * BLOCK, (head + 1) * BLOCK)
                out = (dq_ref[span, :] * SCALE).astype(jnp.bfloat16)
                dq_own[rows, columns(head)] = out[:64]
                dq_sib[rows, columns(head)] = out[64:]
        for at, term in enumerate(terms):
            low = info_ref[4 + at]
            for half in range(2):
                block = low if half == 0 else 15 - low
                place = pl.ds(pl.multiple_of((block + 1) * BLOCK, BLOCK), BLOCK)
                lanes = slice(half * BLOCK, (half + 1) * BLOCK)
                term[group * HEAD : (group + 1) * HEAD, lanes] = (
                    dkt_ref[:, place] * SCALE
                ).astype(jnp.bfloat16)
                term[(GROUPS + group) * HEAD : (GROUPS + group + 1) * HEAD, lanes] = dvt_ref[
                    :, place
                ].astype(jnp.bfloat16)


def attention(info, bounds, q_own, q_sib, c_own, c_sib, chunks, interpret=False):
    vmem = pl.BlockSpec(memory_space=pltpu.VMEM)
    half_rows = jax.ShapeDtypeStruct((128, GROUPS * FOLD * HEAD), jnp.bfloat16)
    term = jax.ShapeDtypeStruct((2 * GROUPS * HEAD, 2 * BLOCK), jnp.bfloat16)
    padded = 2048 + BLOCK
    most = 5
    return pl.pallas_call(
        attention_kernel,
        out_shape=(half_rows,) * 4 + (term,) * 8,
        in_specs=[pl.BlockSpec(memory_space=pltpu.SMEM)] + [vmem] * 13,
        out_specs=(vmem,) * 12,
        scratch_shapes=[
            pltpu.VMEM((GROUPS, padded, HEAD), jnp.bfloat16),
            pltpu.VMEM((GROUPS, padded, HEAD), jnp.bfloat16),
            pltpu.VMEM((ROWS, most * TILE), jnp.float32),
            pltpu.VMEM((ROWS, most * TILE), jnp.bfloat16),
            pltpu.VMEM((ROWS, HEAD), jnp.bfloat16),
            pltpu.VMEM((ROWS, HEAD), jnp.bfloat16),
            pltpu.VMEM((HEAD, ROWS), jnp.bfloat16),
            pltpu.VMEM((HEAD, ROWS), jnp.bfloat16),
            pltpu.VMEM((ROWS, HEAD), jnp.float32),
            pltpu.VMEM((ROWS, HEAD), jnp.float32),
            pltpu.VMEM((ROWS, HEAD), jnp.float32),
            pltpu.VMEM((ROWS, HEAD), jnp.float32),
            pltpu.VMEM((HEAD, padded), jnp.float32),
            pltpu.VMEM((HEAD, padded), jnp.float32),
        ],
        compiler_params=pltpu.CompilerParams(vmem_limit_bytes=40 * 1024 * 1024),
        cost_estimate=pl.CostEstimate(
            flops=6_000_000_000, bytes_accessed=8_000_000, transcendentals=4_000_000
        ),
        interpret=interpret,
    )(info, bounds, q_own, q_sib, c_own, c_sib, *chunks)


def on_device(queries, keys, values, cotangent, live, docs):
    me = lax.axis_index("ctx")
    core = me % 2
    chip = me // 2
    line, side = chip // 2, chip % 2

    def move(shift):
        return [(i, (i + shift) % 16) for i in range(16)]

    def swap(bit):
        return [(i, i ^ bit) for i in range(16)]

    def to_right(a):
        return lax.ppermute(a, "ctx", move(4))

    def to_left(a):
        return lax.ppermute(a, "ctx", move(-4))

    def to_side(a):
        return lax.ppermute(a, "ctx", swap(2))

    def to_core(a):
        return lax.ppermute(a, "ctx", swap(1))

    def part(a, which, width):
        return lax.dynamic_slice_in_dim(a, which * width, width, 1)

    kv_width = GROUPS * HEAD
    kv_send = jnp.concatenate(
        [part(keys[0], 1 - core, kv_width), part(values[0], 1 - core, kv_width)], axis=1
    )
    kv_keep = jnp.concatenate(
        [part(keys[0], core, kv_width), part(values[0], core, kv_width)], axis=1
    )
    kv_got = to_core(kv_send)
    first = jnp.where(core == 0, kv_keep, kv_got)
    second = jnp.where(core == 0, kv_got, kv_keep)
    mine = jnp.concatenate([first[:64], second[:64], second[64:], first[64:]], axis=0)

    from_left = to_right(mine)
    from_right = to_left(mine)
    beside = to_side(mine)
    beside_left = to_right(beside)
    beside_right = to_left(beside)
    opposite = to_right(from_left)
    beside_opposite = to_left(beside_right)
    chunks = (
        mine,
        beside,
        from_right,
        beside_right,
        from_left,
        beside_left,
        opposite,
        beside_opposite,
    )

    q_width = GROUPS * FOLD * HEAD
    q_own, c_own = part(queries[0], core, q_width), part(cotangent[0], core, q_width)
    q_sib = to_core(part(queries[0], 1 - core, q_width))
    c_sib = to_core(part(cotangent[0], 1 - core, q_width))

    own_live = live[0]
    sib_live = to_core(own_live)
    count = jnp.broadcast_to(
        jnp.sum(own_live + sib_live).astype(jnp.float32), (8, 128)
    )
    for bit in (2, 4, 8):
        count = count + lax.ppermute(count, "ctx", swap(bit))
    for bit in (1, 2, 4, 8):
        count = count + lax.ppermute(count, "dp", swap(bit))
    loss_ratio = 32768.0 / count[0, 0]

    offsets = jnp.arange(64, dtype=jnp.int32)
    pieces = [2 * chip + core, 2 * chip + 1 - core, 31 - 2 * chip - core, 30 - 2 * chip + core]
    own_pos = jnp.concatenate([piece * 64 + offsets for piece in pieces])
    row_docs = jnp.concatenate(
        [lax.dynamic_slice_in_dim(docs[0], piece * 64, 64) for piece in pieces]
    )
    low_bound = jnp.sum((docs[0][None, :] < row_docs[:, None]).astype(jnp.int32), axis=1)
    row_live = jnp.concatenate([own_live[:64], sib_live[:64], own_live[64:], sib_live[64:]])
    bounds = jnp.stack([low_bound, own_pos, row_live], axis=1)
    ends = jnp.stack([(chip + 1) * BLOCK, (16 - chip) * BLOCK])
    lows = jnp.stack([jnp.min(low_bound[:128]), jnp.min(low_bound[128:])])
    tiles = (ends - lows + TILE - 1) // TILE
    lines = [line, line, (line + 1) % 4, (line + 1) % 4, (line + 3) % 4, (line + 3) % 4]
    lines += [(line + 2) % 4] * 2
    sides = [side, 1 - side] * 4
    lows_of = jnp.stack([2 * a + b for a, b in zip(lines, sides)])
    info = jnp.concatenate([tiles, ends, lows_of]).astype(jnp.int32)

    results = attention(info, bounds, q_own, q_sib, c_own, c_sib, chunks)
    o_own, o_sib, dq_own, dq_sib = results[:4]
    t_mine, t_beside, t_right, t_beside_right, t_left, t_beside_left, t_opp, t_beside_opp = (
        results[4:]
    )

    def add(*terms):
        return sum(t.astype(jnp.float32) for t in terms).astype(jnp.bfloat16)

    opp_via_right = to_right(t_opp)
    opp_via_left = to_left(t_beside_opp)
    got_beside_1 = to_right(t_beside_right)
    got_mine_1 = to_left(t_left)
    got_mine_2 = to_right(add(t_right, opp_via_right))
    got_beside_2 = to_left(add(t_beside_left, opp_via_left))
    got_side = to_side(add(t_beside, got_beside_1, got_beside_2))
    total = add(t_mine, got_mine_1, got_mine_2, got_side)

    o_got, dq_got = to_core(o_sib), to_core(dq_sib)

    def join(own, got, width):
        low = jnp.where(core == 0, own, got)
        high = jnp.where(core == 0, got, own)
        return jnp.concatenate([low, high], axis=1)

    attended = join(o_own, o_got, q_width)[None]
    grad_queries = (join(dq_own, dq_got, q_width).astype(jnp.float32) * loss_ratio).astype(
        jnp.bfloat16
    )[None]

    token_rows = total.T
    rows_0 = jnp.concatenate([token_rows[:64], token_rows[192:]], axis=0)
    rows_1 = token_rows[64:192]
    kept = jnp.where(core == 0, rows_0, rows_1)
    got = to_core(jnp.where(core == 0, rows_1, rows_0))

    def gradient(at):
        columns = slice(at * kv_width, (at + 1) * kv_width)
        joined = join(kept[:, columns], got[:, columns], kv_width)
        return (joined.astype(jnp.float32) * loss_ratio).astype(jnp.bfloat16)[None]

    return attended, grad_queries, gradient(0), gradient(1)


def solution(mesh):
    rows = P("dp", "ctx", None)
    return jax.shard_map(
        on_device,
        mesh=mesh,
        in_specs=(rows, rows, rows, rows, P("dp", "ctx"), P("dp", None)),
        out_specs=(rows, rows, rows, rows),
        check_vma=False,
    )
```

time: 794 us -> 139 us (0.18); the launches traced: 781 us -> 137 us
  other arithmetic: 222 us -> 11.2 us
  waiting for transfers between devices: 194 us -> 35.6 us
  matrix products: 122 us -> 0 us
  local copies, waits for them, and re-layouts: 147 us -> 26.1 us
  blocking collectives: 77.1 us -> 0 us
  starting transfers between devices: 0.16 us -> 33.5 us
  Pallas kernels: 0 us -> 28.5 us
  between operations: 14.7 us -> 2.31 us
    reduce_scatter x2 -> x0, waiting for transfers between devices: 193 us -> none  [the longest x1 111 us: on_device(): lax.psum_scatter(key_terms.astype(jnp.float32).astype(jnp.bfloat16), 'ctx...]
    add x113 -> x11, other arithmetic: 126 us -> 0.04 us  [the longest x4 0.01 us: on_device(): own_pos = jnp.concatenate([piece * 64 + offsets for piece in pieces])]
    dot_general x112 -> x0, matrix products: 122 us -> none  [the longest x32 37.4 us: tile_scores(): jnp.einsum('qgjd,kgd->gjqk', query_fourfold[query_low:query_high], key_ti...]
    psum x1 -> x0, blocking collectives: 77.1 us -> none  [on_device(): live_count = lax.psum(jnp.sum(live), ('dp', 'ctx'))]
    dynamic_slice x64 -> x4, local copies, waits for them, and re-layouts: 60.1 us -> 4.04 us  [the longest x3 3.96 us: part(): return lax.dynamic_slice_in_dim(a, which * width, width, 1)]
    and x48 -> x0, other arithmetic: 54.7 us -> none  [pair_mask(): (query_doc[query_low:query_high, None] == key_doc[None, key_low:key_high]...]
    ppermute x0 -> x28, waiting for transfers between devices: none -> 35.6 us  [the longest x4 13.8 us: on_device(): count = count + lax.ppermute(count, 'dp', swap(bit))]
    squeeze x49 -> x0, local copies, waits for them, and re-layouts: 34.3 us -> none  [the longest x48 33.1 us: shard_documents(): lax.dynamic_index_in_dim(doc_table, 2 * devices - 1 - shard_index, 0, kee...]
  transfers between devices with their start and end apart: 4 -> 28, of which waited for: 2 -> 10; matrix products, arithmetic and copies ran while one was open for 13% -> 14% of each run, Pallas kernels for 0% -> 21%
where the time goes in v1:
time: 139 us; the launch traced here: 137 us
  waiting for transfers between devices  35.6 us (26%)
  starting transfers between devices  33.5 us (24%)
  Pallas kernels  28.5 us (21%)
  local copies, waits for them, and re-layouts  26.1 us (19%)
  other arithmetic  11.2 us (8%)
  between operations  2.31 us (2%)
    pallas_call x1, Pallas kernels, attention(): pl.pallas_call(attention_kernel, out_shape=(half_rows,) * 4 + (term,) * 8...  28.5 us
    unnamed x54, local copies, waits for them, and re-layouts  15.9 us
    ppermute x4, waiting for transfers between devices, on_device(): count = count + lax.ppermute(count, 'dp', swap(bit))  13.8 us
    ppermute x7, starting transfers between devices, to_core(): return lax.ppermute(a, 'ctx', swap(1))  10.1 us
    ppermute x2, waiting for transfers between devices, to_side(): return lax.ppermute(a, 'ctx', swap(2))  10.1 us
    ppermute x6, starting transfers between devices, to_right(): return lax.ppermute(a, 'ctx', move(4))  9.78 us
    ppermute x4, starting transfers between devices, on_device(): count = count + lax.ppermute(count, 'dp', swap(bit))  6.83 us
    ppermute x6, waiting for transfers between devices, to_right(): return lax.ppermute(a, 'ctx', move(4))  5.4 us
  transfers between devices with their start and end apart: 28, of which 10 were waited for; matrix products, arithmetic and copies ran while one was open for 14% of the time, Pallas kernels for 21%

profile of v1, /device:TPU:31, one launch (start us, length us, event | category | flops | bytes accessed | tf_op | source)
XLA Modules:
  0.0 137.2 jit_solution(1057454806380581572)
XLA Ops:
  2.5 2.1 %dynamic-slice_bitcast_fusion.2 = (bf16[128,2048]{1,0:T(8,128)(2,1)}, bf16[128,2048]{1,0:T(8,128)(2,1)S(1)}) fusion(bf16[1,128,4096]{2,1,0:T(8,128)(2,1)} %param.6, s32[]{:T(128)S(6)} %select_n.141, s32[]{:T(128)S(6)} %select_n.140), kind=kLoop, calls=%fused_computation.11 | loop fusion | bytes 2097160 | tf_op jit(solution)/shard_map/dynamic_slice | solution.py:250
  5.8 1.0 collective-permute-start.4
  8.6 1.3 collective-permute-start.5
  9.9 5.4 %collective-permute-done.4.refs_1_ = bf16[256,512]{1,0:T(8,128)(2,1)S(1)} collective-permute-done((bf16[256,512]{1,0:T(8,128)(2,1)S(1)}, bf16[256,512]{1,0:T(8,128)(2,1)S(1)}, u32[]{:S(2)}, u32[]{:S(2)}) %collective-permute-start.4) | collective-permute-done | bytes 262176 | tf_op jit(solution)/shard_map/ppermute | solution.py:244
  15.9 1.4 %and_select_fusion = s32[2]{0:T(128)S(1)} fusion(s32[1]{0:T(128)} %bitcast.8, s32[1]{0:T(128)} %bitcast.7, s32[1]{0:T(128)} %bitcast.1, s32[1]{0:T(128)} %bitcast), kind=kLoop, calls=%fused_computation.40 | loop fusion | flops 38 | bytes 24 | tf_op jit(solution)/shard_map/jit(floor_divide)/jit(_where)/select_n | solution.py:309
  17.4 1.2 collective-permute-start.2
  18.7 2.1 %collective-permute-start.8 = (bf16[256,512]{1,0:T(8,128)(2,1)S(1)}, bf16[256,512]{1,0:T(8,128)(2,1)}, u32[]{:S(2)}, u32[]{:S(2)}) collective-permute-start(bf16[256,512]{1,0:T(8,128)(2,1)S(1)} %collective-permute-done.4.refs_1_), channel_id=1, source_target_pairs={{0,4},{1,5},{2,6},{3,7},{4,8},{5,9},{6,10},{7,11},{8,12},{9,13},{1... | collective-permute-start | bytes 786440 | tf_op jit(solution)/shard_map/ppermute | solution.py:238
  22.2 1.3 collective-permute-done.6.refs_3_
  26.7 1.6 %collective-permute-start.13 = (f32[8,128]{1,0:T(8,128)S(1)}, f32[8,128]{1,0:T(8,128)S(1)}, u32[]{:S(2)}, u32[]{:S(2)}) collective-permute-start(f32[8,128]{1,0:T(8,128)S(1)} %broadcast_in_dim.5), channel_id=1, source_target_pairs={{0,2},{1,3},{2,0},{3,1},{4,6},{5,7},{6,4},{7,5},{8,10},{9,11},{10,... | collective-permute-start | bytes 12296 | tf_op jit(solution)/shard_map/ppermute | solution.py:293
  29.1 3.2 %collective-permute-done.9.refs_6_ = bf16[256,512]{1,0:T(8,128)(2,1)S(1)} collective-permute-done((bf16[256,512]{1,0:T(8,128)(2,1)S(1)}, bf16[256,512]{1,0:T(8,128)(2,1)S(1)}, u32[]{:S(2)}, u32[]{:S(2)}) %collective-permute-start.9) | collective-permute-done | bytes 262176 | tf_op jit(solution)/shard_map/ppermute | solution.py:238
  34.1 1.0 copy-done.13
  39.9 28.5 %shard_map.93 = (bf16[128,2048]{1,0:T(8,128)(2,1)S(1)}, bf16[128,2048]{1,0:T(8,128)(2,1)S(1)}, bf16[128,2048]{1,0:T(8,128)(2,1)S(1)}, bf16[128,2048]{1,0:T(8,128...) custom-call(s32[12]{0:T(128)S(1)} %concatenate.71.info_ref, ...), custom_call_target="tpu_custom_call" | custom-call | flops 6000000000 | bytes 8000000 | tf_op jit(solution)/shard_map/pallas_call | solution.py:196
  72.8 1.9 %copy.46 = bf16[512,256]{0,1:T(8,128)(2,1)} copy(bf16[512,256]{1,0:T(8,128)(2,1)} %copy-done.5) | data formatting | bytes 524288 | tf_op jit(solution)/shard_map/pallas_call | solution.py:196
  74.9 5.0 %collective-permute-done.14 = f32[8,128]{1,0:T(8,128)S(1)} collective-permute-done((f32[8,128]{1,0:T(8,128)S(1)}, f32[8,128]{1,0:T(8,128)S(1)}, u32[]{:S(2)}, u32[]{:S(2)}) %collective-permute-start.14) | collective-permute-done | bytes 4128 | tf_op jit(solution)/shard_map/ppermute | solution.py:293
  80.0 1.8 %copy.42 = bf16[512,256]{0,1:T(8,128)(2,1)} copy(bf16[512,256]{1,0:T(8,128)(2,1)} %copy-done.4) | data formatting | bytes 524288 | tf_op jit(solution)/shard_map/pallas_call | solution.py:196
  82.8 4.7 %collective-permute-start.21 = (bf16[512,256]{0,1:T(8,128)(2,1)}, bf16[512,256]{0,1:T(8,128)(2,1)}, u32[]{:S(2)}, u32[]{:S(2)}) collective-permute-start(bf16[512,256]{0,1:T(8,128)(2,1)} %copy.42), channel_id=1, source_target_pairs={{0,4},{1,5},{2,6},{3,7},{4,8},{5,9},{6,10},{7,11},{8,12},{9,13},{1... | collective-permute-start | bytes 786440 | tf_op jit(solution)/shard_map/ppermute | solution.py:238
  87.5 2.3 %collective-permute-start.11 = (bf16[128,2048]{1,0:T(8,128)(2,1)S(1)}, bf16[128,2048]{1,0:T(8,128)(2,1)}, u32[]{:S(2)}, u32[]{:S(2)}) collective-permute-start(bf16[128,2048]{1,0:T(8,128)(2,1)S(1)} %copy-done.11), channel_id=1, source_target_pairs={{0,1},{1,0},{2,3},{3,2},{4,5},{5,4},{6,7},{7,6},{8,9},{9,8},{10,11... | collective-permute-start | bytes 1572872 | tf_op jit(solution)/shard_map/ppermute | solution.py:247
  90.6 1.7 %collective-permute-start.25 = (bf16[512,256]{0,1:T(8,128)(2,1)}, bf16[512,256]{0,1:T(8,128)(2,1)}, u32[]{:S(2)}, u32[]{:S(2)}) collective-permute-start(bf16[512,256]{0,1:T(8,128)(2,1)} %add_convert_fusion.2), channel_id=1, source_target_pairs={{0,12},{1,13},{2,14},{3,15},{4,0},{5,1},{6,2},{7,3},{8,4},{9,5},{1... | collective-permute-start | bytes 786440 | tf_op jit(solution)/shard_map/ppermute | solution.py:241
  92.3 6.8 %collective-permute-start.16 = (f32[8,128]{1,0:T(8,128)S(1)}, f32[8,128]{1,0:T(8,128)S(1)}, u32[]{:S(2)}, u32[]{:S(2)}) collective-permute-start(f32[8,128]{1,0:T(8,128)S(1)} %add.208), channel_id=1, source_target_pairs={{0,16},{16,0},{32,48},{48,32},{64,80},{80,64},{96,112},{112,96},{1... | collective-permute-start | bytes 12296 | tf_op jit(solution)/shard_map/ppermute | solution.py:295
  99.1 1.4 collective-permute-done.16
  100.5 3.4 %collective-permute-done.17 = f32[8,128]{1,0:T(8,128)S(1)} collective-permute-done((f32[8,128]{1,0:T(8,128)S(1)}, f32[8,128]{1,0:T(8,128)S(1)}, u32[]{:S(2)}, u32[]{:S(2)}) %collective-permute-start.17) | collective-permute-done | bytes 4128 | tf_op jit(solution)/shard_map/ppermute | solution.py:295
  103.8 6.4 %collective-permute-done.18 = f32[8,128]{1,0:T(8,128)S(1)} collective-permute-done((f32[8,128]{1,0:T(8,128)S(1)}, f32[8,128]{1,0:T(8,128)S(1)}, u32[]{:S(2)}, u32[]{:S(2)}) %collective-permute-start.18) | collective-permute-done | bytes 4128 | tf_op jit(solution)/shard_map/ppermute | solution.py:295
  110.2 2.7 %collective-permute-done.19 = f32[8,128]{1,0:T(8,128)S(1)} collective-permute-done((f32[8,128]{1,0:T(8,128)S(1)}, f32[8,128]{1,0:T(8,128)S(1)}, u32[]{:S(2)}, u32[]{:S(2)}) %collective-permute-start.19) | collective-permute-done | bytes 4128 | tf_op jit(solution)/shard_map/ppermute | solution.py:295
  115.1 4.0 %collective-permute-start.12 = (bf16[128,2048]{1,0:T(8,128)(2,1)S(1)}, bf16[128,2048]{1,0:T(8,128)(2,1)S(1)}, u32[]{:S(2)}, u32[]{:S(2)}) collective-permute-start(bf16[128,2048]{1,0:T(8,128)(2,1)S(1)} %copy-done.9), channel_id=1, source_target_pairs={{0,1},{1,0},{2,3},{3,2},{4,5},{5,4},{6,7},{7,6},{8,9},{9,8},{10,11... | collective-permute-start | bytes 1572872 | tf_op jit(solution)/shard_map/ppermute | solution.py:247
  120.2 2.7 %collective-permute-start.22 = (bf16[512,256]{0,1:T(8,128)(2,1)S(1)}, bf16[512,256]{0,1:T(8,128)(2,1)S(1)}, u32[]{:S(2)}, u32[]{:S(2)}) collective-permute-start(bf16[512,256]{0,1:T(8,128)(2,1)S(1)} %add_convert_fusion.3), channel_id=1, source_target_pairs={{0,4},{1,5},{2,6},{3,7},{4,8},{5,9},{6,10},{7,11},{8,12},{9,13},{1... | collective-permute-start | bytes 786440 | tf_op jit(solution)/shard_map/ppermute | solution.py:238
  122.8 1.1 add_convert_fusion.1
  124.1 1.1 broadcast_select_fusion.1
  125.3 1.1 maximum_bitcast_fusion
  126.4 2.2 %collective-permute-done.22 = bf16[512,256]{0,1:T(8,128)(2,1)S(1)} collective-permute-done((bf16[512,256]{0,1:T(8,128)(2,1)S(1)}, bf16[512,256]{0,1:T(8,128)(2,1)S(1)}, u32[]{:S(2)}, u32[]{:S(2)}) %collective-permute-start.22) | collective-permute-done | bytes 262176 | tf_op jit(solution)/shard_map/ppermute | solution.py:238
  128.6 4.6 %collective-permute-done.26 = bf16[512,256]{0,1:T(8,128)(2,1)S(1)} collective-permute-done((bf16[512,256]{0,1:T(8,128)(2,1)S(1)}, bf16[512,256]{0,1:T(8,128)(2,1)S(1)}, u32[]{:S(2)}, u32[]{:S(2)}) %collective-permute-start.26) | collective-permute-done | bytes 262176 | tf_op jit(solution)/shard_map/ppermute | solution.py:244
  133.4 1.2 collective-permute-start.27
  134.6 1.2 multiply_convert_fusion
  (132 shorter events, 27.5 us)
Async XLA Ops:
  0.6 16.7 %collective-permute-start = (s32[128]{0:T(128)}, s32[128]{0:T(128)S(1)}, u32[]{:S(2)}, u32[]{:S(2)}) collective-permute-start(s32[128]{0:T(128)} %bitcast.67), channel_id=1, source_target_pairs={{0,1},{1,0},{2,3},{3,2},{4,5},{5,4},{6,7},{7,6},{8,9},{9,8},{10,11... | collective-permute-start | bytes 1544 | tf_op jit(solution)/shard_map/ppermute | solution.py:247
  2.4 3.4 %collective-permute-start.3 = (bf16[128,512]{1,0:T(8,128)(2,1)S(1)}, bf16[128,512]{1,0:T(8,128)(2,1)S(1)}, u32[]{:S(2)}, u32[]{:S(2)}) collective-permute-start(bf16[128,512]{1,0:T(8,128)(2,1)S(1)} %pad_maximum_fusion.2), channel_id=1, source_target_pairs={{0,1},{1,0},{2,3},{3,2},{4,5},{5,4},{6,7},{7,6},{8,9},{9,8},{10,11... | collective-permute-start | bytes 393224 | tf_op jit(solution)/shard_map/ppermute | solution.py:247
  4.6 21.3 %collective-permute-start.1 = (bf16[128,2048]{1,0:T(8,128)(2,1)}, bf16[128,2048]{1,0:T(8,128)(2,1)S(1)}, u32[]{:S(2)}, u32[]{:S(2)}) collective-permute-start(bf16[128,2048]{1,0:T(8,128)(2,1)} %get-tuple-element.36), channel_id=1, source_target_pairs={{0,1},{1,0},{2,3},{3,2},{4,5},{5,4},{6,7},{7,6},{8,9},{9,8},{10,11... | collective-permute-start | bytes 1572872 | tf_op jit(solution)/shard_map/ppermute | solution.py:247
  5.8 9.5 %collective-permute-start.4 = (bf16[256,512]{1,0:T(8,128)(2,1)S(1)}, bf16[256,512]{1,0:T(8,128)(2,1)S(1)}, u32[]{:S(2)}, u32[]{:S(2)}) collective-permute-start(bf16[256,512]{1,0:T(8,128)(2,1)S(1)} %pad_maximum_fusion.refs_0_), channel_id=1, source_target_pairs={{0,2},{1,3},{2,0},{3,1},{4,6},{5,7},{6,4},{7,5},{8,10},{9,11},{10,... | collective-permute-start | bytes 786440 | tf_op jit(solution)/shard_map/ppermute | solution.py:244
  8.4 10.3 %collective-permute-start.7 = (bf16[256,512]{1,0:T(8,128)(2,1)S(1)}, bf16[256,512]{1,0:T(8,128)(2,1)S(1)}, u32[]{:S(2)}, u32[]{:S(2)}) collective-permute-start(bf16[256,512]{1,0:T(8,128)(2,1)S(1)} %pad_maximum_fusion.refs_0_), channel_id=1, source_target_pairs={{0,4},{1,5},{2,6},{3,7},{4,8},{5,9},{6,10},{7,11},{8,12},{9,13},{1... | collective-permute-start | bytes 786440 | tf_op jit(solution)/shard_map/ppermute | solution.py:238
  8.6 12.2 %collective-permute-start.5 = (bf16[256,512]{1,0:T(8,128)(2,1)S(1)}, bf16[256,512]{1,0:T(8,128)(2,1)S(1)}, u32[]{:S(2)}, u32[]{:S(2)}) collective-permute-start(bf16[256,512]{1,0:T(8,128)(2,1)S(1)} %pad_maximum_fusion.refs_0_), channel_id=1, source_target_pairs={{0,12},{1,13},{2,14},{3,15},{4,0},{5,1},{6,2},{7,3},{8,4},{9,5},{1... | collective-permute-start | bytes 786440 | tf_op jit(solution)/shard_map/ppermute | solution.py:241
  15.3 17.7 %copy-start.14 = (bf16[256,512]{1,0:T(8,128)(2,1)}, bf16[256,512]{1,0:T(8,128)(2,1)S(1)}, u32[]{:S(2)}) copy-start(bf16[256,512]{1,0:T(8,128)(2,1)S(1)} %collective-permute-done.4.refs_1_) | copy-start | bytes 786436
  15.3 8.2 %collective-permute-start.6 = (bf16[256,512]{1,0:T(8,128)(2,1)S(1)}, bf16[256,512]{1,0:T(8,128)(2,1)S(1)}, u32[]{:S(2)}, u32[]{:S(2)}) collective-permute-start(bf16[256,512]{1,0:T(8,128)(2,1)S(1)} %collective-permute-done.4.refs_1_), channel_id=1, source_target_pairs={{0,12},{1,13},{2,14},{3,15},{4,0},{5,1},{6,2},{7,3},{8,4},{9,5},{1... | collective-permute-start | bytes 786440 | tf_op jit(solution)/shard_map/ppermute | solution.py:241
  17.4 10.9 %collective-permute-start.2 = (bf16[128,2048]{1,0:T(8,128)(2,1)}, bf16[128,2048]{1,0:T(8,128)(2,1)S(1)}, u32[]{:S(2)}, u32[]{:S(2)}) collective-permute-start(bf16[128,2048]{1,0:T(8,128)(2,1)} %get-tuple-element.34), channel_id=1, source_target_pairs={{0,1},{1,0},{2,3},{3,2},{4,5},{5,4},{6,7},{7,6},{8,9},{9,8},{10,11... | collective-permute-start | bytes 1572872 | tf_op jit(solution)/shard_map/ppermute | solution.py:247
  18.7 14.3 %collective-permute-start.8 = (bf16[256,512]{1,0:T(8,128)(2,1)S(1)}, bf16[256,512]{1,0:T(8,128)(2,1)}, u32[]{:S(2)}, u32[]{:S(2)}) collective-permute-start(bf16[256,512]{1,0:T(8,128)(2,1)S(1)} %collective-permute-done.4.refs_1_), channel_id=1, source_target_pairs={{0,4},{1,5},{2,6},{3,7},{4,8},{5,9},{6,10},{7,11},{8,12},{9,13},{1... | collective-permute-start | bytes 786440 | tf_op jit(solution)/shard_map/ppermute | solution.py:238
  21.5 10.8 %collective-permute-start.9 = (bf16[256,512]{1,0:T(8,128)(2,1)S(1)}, bf16[256,512]{1,0:T(8,128)(2,1)S(1)}, u32[]{:S(2)}, u32[]{:S(2)}) collective-permute-start(bf16[256,512]{1,0:T(8,128)(2,1)S(1)} %collective-permute-done.7.refs_4_), channel_id=1, source_target_pairs={{0,4},{1,5},{2,6},{3,7},{4,8},{5,9},{6,10},{7,11},{8,12},{9,13},{1... | collective-permute-start | bytes 786440 | tf_op jit(solution)/shard_map/ppermute | solution.py:238
  23.5 9.5 %collective-permute-start.10 = (bf16[256,512]{1,0:T(8,128)(2,1)S(1)}, bf16[256,512]{1,0:T(8,128)(2,1)}, u32[]{:S(2)}, u32[]{:S(2)}) collective-permute-start(bf16[256,512]{1,0:T(8,128)(2,1)S(1)} %collective-permute-done.6.refs_3_), channel_id=1, source_target_pairs={{0,12},{1,13},{2,14},{3,15},{4,0},{5,1},{6,2},{7,3},{8,4},{9,5},{1... | collective-permute-start | bytes 786440 | tf_op jit(solution)/shard_map/ppermute | solution.py:241
  26.7 48.1 %collective-permute-start.13 = (f32[8,128]{1,0:T(8,128)S(1)}, f32[8,128]{1,0:T(8,128)S(1)}, u32[]{:S(2)}, u32[]{:S(2)}) collective-permute-start(f32[8,128]{1,0:T(8,128)S(1)} %broadcast_in_dim.5), channel_id=1, source_target_pairs={{0,2},{1,3},{2,0},{3,1},{4,6},{5,7},{6,4},{7,5},{8,10},{9,11},{10,... | collective-permute-start | bytes 12296 | tf_op jit(solution)/shard_map/ppermute | solution.py:293
  72.8 9.0 %copy-start.3 = (bf16[512,256]{1,0:T(8,128)(2,1)S(1)}, bf16[512,256]{1,0:T(8,128)(2,1)}, u32[]{:S(2)}) copy-start(bf16[512,256]{1,0:T(8,128)(2,1)} %copy-done.2) | copy-start | bytes 786436
  72.8 9.8 %copy-start.1 = (bf16[512,256]{1,0:T(8,128)(2,1)S(1)}, bf16[512,256]{1,0:T(8,128)(2,1)}, u32[]{:S(2)}) copy-start(bf16[512,256]{1,0:T(8,128)(2,1)} %copy-done) | copy-start | bytes 786436
  72.8 14.7 %copy-start.11 = (bf16[128,2048]{1,0:T(8,128)(2,1)S(1)}, bf16[128,2048]{1,0:T(8,128)(2,1)}, u32[]{:S(2)}) copy-start(bf16[128,2048]{1,0:T(8,128)(2,1)} %copy-done.10) | copy-start | bytes 1572868
  74.7 15.1 %collective-permute-start.24 = (bf16[512,256]{0,1:T(8,128)(2,1)}, bf16[512,256]{0,1:T(8,128)(2,1)S(1)}, u32[]{:S(2)}, u32[]{:S(2)}) collective-permute-start(bf16[512,256]{0,1:T(8,128)(2,1)} %copy.46), channel_id=1, source_target_pairs={{0,12},{1,13},{2,14},{3,15},{4,0},{5,1},{6,2},{7,3},{8,4},{9,5},{1... | collective-permute-start | bytes 786440 | tf_op jit(solution)/shard_map/ppermute | solution.py:241
  74.8 5.1 %collective-permute-start.14 = (f32[8,128]{1,0:T(8,128)S(1)}, f32[8,128]{1,0:T(8,128)S(1)}, u32[]{:S(2)}, u32[]{:S(2)}) collective-permute-start(f32[8,128]{1,0:T(8,128)S(1)} %broadcast_add_fusion), channel_id=1, source_target_pairs={{0,4},{1,5},{2,6},{3,7},{4,0},{5,1},{6,2},{7,3},{8,12},{9,13},{10,... | collective-permute-start | bytes 12296 | tf_op jit(solution)/shard_map/ppermute | solution.py:293
  80.0 12.3 %collective-permute-start.15 = (f32[8,128]{1,0:T(8,128)S(1)}, f32[8,128]{1,0:T(8,128)S(1)}, u32[]{:S(2)}, u32[]{:S(2)}) collective-permute-start(f32[8,128]{1,0:T(8,128)S(1)} %fusion.9), channel_id=1, source_target_pairs={{0,8},{1,9},{2,10},{3,11},{4,12},{5,13},{6,14},{7,15},{8,0},{9,1},... | collective-permute-start | bytes 12296 | tf_op jit(solution)/shard_map/ppermute | solution.py:293
  82.8 32.1 %collective-permute-start.21 = (bf16[512,256]{0,1:T(8,128)(2,1)}, bf16[512,256]{0,1:T(8,128)(2,1)}, u32[]{:S(2)}, u32[]{:S(2)}) collective-permute-start(bf16[512,256]{0,1:T(8,128)(2,1)} %copy.42), channel_id=1, source_target_pairs={{0,4},{1,5},{2,6},{3,7},{4,8},{5,9},{6,10},{7,11},{8,12},{9,13},{1... | collective-permute-start | bytes 786440 | tf_op jit(solution)/shard_map/ppermute | solution.py:238
  87.4 32.7 %collective-permute-start.23 = (bf16[512,256]{0,1:T(8,128)(2,1)}, bf16[512,256]{0,1:T(8,128)(2,1)}, u32[]{:S(2)}, u32[]{:S(2)}) collective-permute-start(bf16[512,256]{0,1:T(8,128)(2,1)} %copy.44), channel_id=1, source_target_pairs={{0,4},{1,5},{2,6},{3,7},{4,8},{5,9},{6,10},{7,11},{8,12},{9,13},{1... | collective-permute-start | bytes 786440 | tf_op jit(solution)/shard_map/ppermute | solution.py:238
  87.5 36.6 %collective-permute-start.11 = (bf16[128,2048]{1,0:T(8,128)(2,1)S(1)}, bf16[128,2048]{1,0:T(8,128)(2,1)}, u32[]{:S(2)}, u32[]{:S(2)}) collective-permute-start(bf16[128,2048]{1,0:T(8,128)(2,1)S(1)} %copy-done.11), channel_id=1, source_target_pairs={{0,1},{1,0},{2,3},{3,2},{4,5},{5,4},{6,7},{7,6},{8,9},{9,8},{10,11... | collective-permute-start | bytes 1572872 | tf_op jit(solution)/shard_map/ppermute | solution.py:247
  90.6 32.2 %collective-permute-start.25 = (bf16[512,256]{0,1:T(8,128)(2,1)}, bf16[512,256]{0,1:T(8,128)(2,1)}, u32[]{:S(2)}, u32[]{:S(2)}) collective-permute-start(bf16[512,256]{0,1:T(8,128)(2,1)} %add_convert_fusion.2), channel_id=1, source_target_pairs={{0,12},{1,13},{2,14},{3,15},{4,0},{5,1},{6,2},{7,3},{8,4},{9,5},{1... | collective-permute-start | bytes 786440 | tf_op jit(solution)/shard_map/ppermute | solution.py:241
  92.3 8.2 %collective-permute-start.16 = (f32[8,128]{1,0:T(8,128)S(1)}, f32[8,128]{1,0:T(8,128)S(1)}, u32[]{:S(2)}, u32[]{:S(2)}) collective-permute-start(f32[8,128]{1,0:T(8,128)S(1)} %add.208), channel_id=1, source_target_pairs={{0,16},{16,0},{32,48},{48,32},{64,80},{80,64},{96,112},{112,96},{1... | collective-permute-start | bytes 12296 | tf_op jit(solution)/shard_map/ppermute | solution.py:295
  100.5 3.4 %collective-permute-start.17 = (f32[8,128]{1,0:T(8,128)S(1)}, f32[8,128]{1,0:T(8,128)S(1)}, u32[]{:S(2)}, u32[]{:S(2)}) collective-permute-start(f32[8,128]{1,0:T(8,128)S(1)} %add.209), channel_id=1, source_target_pairs={{0,32},{16,48},{32,0},{48,16},{64,96},{80,112},{96,64},{112,80},{1... | collective-permute-start | bytes 12296 | tf_op jit(solution)/shard_map/ppermute | solution.py:295
  103.8 6.4 %collective-permute-start.18 = (f32[8,128]{1,0:T(8,128)S(1)}, f32[8,128]{1,0:T(8,128)S(1)}, u32[]{:S(2)}, u32[]{:S(2)}) collective-permute-start(f32[8,128]{1,0:T(8,128)S(1)} %add.210), channel_id=1, source_target_pairs={{0,64},{16,80},{32,96},{48,112},{64,0},{80,16},{96,32},{112,48},{1... | collective-permute-start | bytes 12296 | tf_op jit(solution)/shard_map/ppermute | solution.py:295
  110.2 2.7 %collective-permute-start.19 = (f32[8,128]{1,0:T(8,128)S(1)}, f32[8,128]{1,0:T(8,128)S(1)}, u32[]{:S(2)}, u32[]{:S(2)}) collective-permute-start(f32[8,128]{1,0:T(8,128)S(1)} %add.211), channel_id=1, source_target_pairs={{0,128},{16,144},{32,160},{48,176},{64,192},{80,208},{96,224},{112... | collective-permute-start | bytes 12296 | tf_op jit(solution)/shard_map/ppermute | solution.py:295
  114.7 11.7 %collective-permute-start.20 = (bf16[512,256]{0,1:T(8,128)(2,1)S(1)}, bf16[512,256]{0,1:T(8,128)(2,1)S(1)}, u32[]{:S(2)}, u32[]{:S(2)}) collective-permute-start(bf16[512,256]{0,1:T(8,128)(2,1)S(1)} %copy.40), channel_id=1, source_target_pairs={{0,12},{1,13},{2,14},{3,15},{4,0},{5,1},{6,2},{7,3},{8,4},{9,5},{1... | collective-permute-start | bytes 786440 | tf_op jit(solution)/shard_map/ppermute | solution.py:241
  115.1 10.1 %collective-permute-start.12 = (bf16[128,2048]{1,0:T(8,128)(2,1)S(1)}, bf16[128,2048]{1,0:T(8,128)(2,1)S(1)}, u32[]{:S(2)}, u32[]{:S(2)}) collective-permute-start(bf16[128,2048]{1,0:T(8,128)(2,1)S(1)} %copy-done.9), channel_id=1, source_target_pairs={{0,1},{1,0},{2,3},{3,2},{4,5},{5,4},{6,7},{7,6},{8,9},{9,8},{10,11... | collective-permute-start | bytes 1572872 | tf_op jit(solution)/shard_map/ppermute | solution.py:247
  120.2 8.4 %collective-permute-start.22 = (bf16[512,256]{0,1:T(8,128)(2,1)S(1)}, bf16[512,256]{0,1:T(8,128)(2,1)S(1)}, u32[]{:S(2)}, u32[]{:S(2)}) collective-permute-start(bf16[512,256]{0,1:T(8,128)(2,1)S(1)} %add_convert_fusion.3), channel_id=1, source_target_pairs={{0,4},{1,5},{2,6},{3,7},{4,8},{5,9},{6,10},{7,11},{8,12},{9,13},{1... | collective-permute-start | bytes 786440 | tf_op jit(solution)/shard_map/ppermute | solution.py:238
  124.0 9.2 %collective-permute-start.26 = (bf16[512,256]{0,1:T(8,128)(2,1)S(1)}, bf16[512,256]{0,1:T(8,128)(2,1)S(1)}, u32[]{:S(2)}, u32[]{:S(2)}) collective-permute-start(bf16[512,256]{0,1:T(8,128)(2,1)S(1)} %add_convert_fusion.1), channel_id=1, source_target_pairs={{0,2},{1,3},{2,0},{3,1},{4,6},{5,7},{6,4},{7,5},{8,10},{9,11},{10,... | collective-permute-start | bytes 786440 | tf_op jit(solution)/shard_map/ppermute | solution.py:244
  133.4 2.4 %collective-permute-start.27 = (bf16[128,512]{1,0:T(8,128)(2,1)S(1)}, bf16[128,512]{1,0:T(8,128)(2,1)S(1)}, u32[]{:S(2)}, u32[]{:S(2)}) collective-permute-start(bf16[128,512]{1,0:T(8,128)(2,1)S(1)} %get-tuple-element.39), channel_id=1, source_target_pairs={{0,1},{1,0},{2,3},{3,2},{4,5},{5,4},{6,7},{7,6},{8,9},{9,8},{10,11... | collective-permute-start | bytes 393224 | tf_op jit(solution)/shard_map/ppermute | solution.py:247
  (23 other events, 24.9 us)

commit v2 on v1

--- a/solution.py
+++ b/solution.py
@@ -17,6 +17,9 @@
 MASKED = -1e30
 SCALE = 1.0 / math.sqrt(HEAD)
 SCALE_LOG2E = SCALE * math.log2(math.e)
+
+TERM_ROWS = 2 * GROUPS * HEAD + 16
+DIGIT = 32
 
 NT = (((1,), (1,)), ((), ()))
 NN = (((1,), (0,)), ((), ()))
@@ -175,6 +178,14 @@
                 dq_sib[rows, columns(head)] = out[64:]
         for at, term in enumerate(terms):
             low = info_ref[4 + at]
+            if group == 0:
+                digit_row = lax.broadcasted_iota(jnp.int32, (16, 2 * BLOCK), 0)
+                digits = jnp.zeros((16, 2 * BLOCK), jnp.float32)
+                for place in range(3):
+                    digits = jnp.where(
+                        digit_row == place, info_ref[12 + place].astype(jnp.float32), digits
+                    )
+                term[2 * GROUPS * HEAD :, :] = digits.astype(jnp.bfloat16)
             for half in range(2):
                 block = low if half == 0 else 15 - low
                 place = pl.ds(pl.multiple_of((block + 1) * BLOCK, BLOCK), BLOCK)
@@ -190,7 +201,7 @@
 def attention(info, bounds, q_own, q_sib, c_own, c_sib, chunks, interpret=False):
     vmem = pl.BlockSpec(memory_space=pltpu.VMEM)
     half_rows = jax.ShapeDtypeStruct((128, GROUPS * FOLD * HEAD), jnp.bfloat16)
-    term = jax.ShapeDtypeStruct((2 * GROUPS * HEAD, 2 * BLOCK), jnp.bfloat16)
+    term = jax.ShapeDtypeStruct((TERM_ROWS, 2 * BLOCK), jnp.bfloat16)
     padded = 2048 + BLOCK
     most = 5
     return pl.pallas_call(
@@ -214,12 +225,41 @@
             pltpu.VMEM((HEAD, padded), jnp.float32),
             pltpu.VMEM((HEAD, padded), jnp.float32),
         ],
-        compiler_params=pltpu.CompilerParams(vmem_limit_bytes=40 * 1024 * 1024),
+        compiler_params=pltpu.CompilerParams(vmem_limit_bytes=20 * 1024 * 1024),
         cost_estimate=pl.CostEstimate(
             flops=6_000_000_000, bytes_accessed=8_000_000, transcendentals=4_000_000
         ),
         interpret=interpret,
     )(info, bounds, q_own, q_sib, c_own, c_sib, *chunks)
+
+
+def closing_kernel(info_ref, *refs):
+    terms, (kept, sent, ratio) = refs[:4], refs[4:]
+    total = sum(term[...].astype(jnp.float32) for term in terms)
+    width = 2 * GROUPS * HEAD
+    digits = total[width : width + 8, :HEAD]
+    count = digits[0:1] + DIGIT * (digits[1:2] + DIGIT * digits[2:3])
+    ratio_row = 32768.0 / count
+    ratio[...] = jnp.broadcast_to(ratio_row, (8, HEAD))
+    rows = (total[:width] * ratio_row[:, :1]).T
+    outer = jnp.concatenate([rows[:64], rows[192:]], axis=0).astype(jnp.bfloat16)
+    inner = rows[64:192].astype(jnp.bfloat16)
+    first = info_ref[0] == 0
+    kept[...] = jnp.where(first, outer, inner)
+    sent[...] = jnp.where(first, inner, outer)
+
+
+def closing(info, terms):
+    vmem = pl.BlockSpec(memory_space=pltpu.VMEM)
+    rows = jax.ShapeDtypeStruct((BLOCK, 2 * GROUPS * HEAD), jnp.bfloat16)
+    return pl.pallas_call(
+        closing_kernel,
+        out_shape=(rows, rows, jax.ShapeDtypeStruct((8, HEAD), jnp.float32)),
+        in_specs=[pl.BlockSpec(memory_space=pltpu.SMEM)] + [vmem] * 4,
+        out_specs=(vmem,) * 3,
+        compiler_params=pltpu.CompilerParams(vmem_limit_bytes=8 * 1024 * 1024),
+        cost_estimate=pl.CostEstimate(flops=1_000_000, bytes_accessed=1_000_000, transcendentals=0),
+    )(info, *terms)
 
 
 def on_device(queries, keys, values, cotangent, live, docs):
@@ -279,21 +319,20 @@
         beside_opposite,
     )
 
+    own_live = live[0]
+    sib_live = to_core(own_live)
+    count = jnp.broadcast_to(jnp.sum(own_live + sib_live).astype(jnp.float32), (8, 128))
+    for bit in (1, 2):
+        count = count + lax.ppermute(count, "dp", swap(bit))
+    queries, cotangent, count, _ = lax.optimization_barrier((queries, cotangent, count, beside))
+    for bit in (4, 8):
+        count = count + lax.ppermute(count, "dp", swap(bit))
+    chip_count = count[0, 0].astype(jnp.int32)
+
     q_width = GROUPS * FOLD * HEAD
-    q_own, c_own = part(queries[0], core, q_width), part(cotangent[0], core, q_width)
     q_sib = to_core(part(queries[0], 1 - core, q_width))
     c_sib = to_core(part(cotangent[0], 1 - core, q_width))
-
-    own_live = live[0]
-    sib_live = to_core(own_live)
-    count = jnp.broadcast_to(
-        jnp.sum(own_live + sib_live).astype(jnp.float32), (8, 128)
-    )
-    for bit in (2, 4, 8):
-        count = count + lax.ppermute(count, "ctx", swap(bit))
-    for bit in (1, 2, 4, 8):
-        count = count + lax.ppermute(count, "dp", swap(bit))
-    loss_ratio = 32768.0 / count[0, 0]
+    q_own, c_own = part(queries[0], core, q_width), part(cotangent[0], core, q_width)
 
     offsets = jnp.arange(64, dtype=jnp.int32)
     pieces = [2 * chip + core, 2 * chip + 1 - core, 31 - 2 * chip - core, 30 - 2 * chip + core]
@@ -311,7 +350,10 @@
     lines += [(line + 2) % 4] * 2
     sides = [side, 1 - side] * 4
     lows_of = jnp.stack([2 * a + b for a, b in zip(lines, sides)])
-    info = jnp.concatenate([tiles, ends, lows_of]).astype(jnp.int32)
+    digits = jnp.stack(
+        [chip_count % DIGIT, chip_count // DIGIT % DIGIT, chip_count // (DIGIT * DIGIT)]
+    )
+    info = jnp.concatenate([tiles, ends, lows_of, digits]).astype(jnp.int32)
 
     results = attention(info, bounds, q_own, q_sib, c_own, c_sib, chunks)
     o_own, o_sib, dq_own, dq_sib = results[:4]
@@ -329,7 +371,10 @@
     got_mine_2 = to_right(add(t_right, opp_via_right))
     got_beside_2 = to_left(add(t_beside_left, opp_via_left))
     got_side = to_side(add(t_beside, got_beside_1, got_beside_2))
-    total = add(t_mine, got_mine_1, got_mine_2, got_side)
+    kept, sent, ratio = closing(
+        core.reshape(1).astype(jnp.int32), (t_mine, got_mine_1, got_mine_2, got_side)
+    )
+    got = to_core(sent)
 
     o_got, dq_got = to_core(o_sib), to_core(dq_sib)
 
@@ -339,20 +384,13 @@
         return jnp.concatenate([low, high], axis=1)
 
     attended = join(o_own, o_got, q_width)[None]
-    grad_queries = (join(dq_own, dq_got, q_width).astype(jnp.float32) * loss_ratio).astype(
+    grad_queries = (join(dq_own, dq_got, q_width).astype(jnp.float32) * ratio[0, 0]).astype(
         jnp.bfloat16
     )[None]
 
-    token_rows = total.T
-    rows_0 = jnp.concatenate([token_rows[:64], token_rows[192:]], axis=0)
-    rows_1 = token_rows[64:192]
-    kept = jnp.where(core == 0, rows_0, rows_1)
-    got = to_core(jnp.where(core == 0, rows_1, rows_0))
-
     def gradient(at):
         columns = slice(at * kv_width, (at + 1) * kv_width)
-        joined = join(kept[:, columns], got[:, columns], kv_width)
-        return (joined.astype(jnp.float32) * loss_ratio).astype(jnp.bfloat16)[None]
+        return join(kept[:, columns], got[:, columns], kv_width)[None]
 
     return attended, grad_queries, gradient(0), gradient(1)
 

time: 139 us -> 115 us (0.83)
  the two profiles are of different devices: /device:TPU:31 before, /device:TPU:1 now
where the time goes in v2:
time: 115 us
  starting transfers between devices  46.7 us (41%)
  waiting for transfers between devices  30.8 us (27%)
  Pallas kernels  18.1 us (16%)
  other arithmetic  10.3 us (9%)
  local copies, waits for them, and re-layouts  6.88 us (6%)
  between operations  2.22 us (2%)
    pallas_call x1, Pallas kernels, attention(): pl.pallas_call(attention_kernel, out_shape=(half_rows,) * 4 + (term,) * 8...  17.9 us
    ppermute x6, starting transfers between devices, to_right(): return lax.ppermute(a, 'ctx', move(4))  13.3 us
    ppermute x7, starting transfers between devices, to_core(): return lax.ppermute(a, 'ctx', swap(1))  13.2 us
    ppermute x6, waiting for transfers between devices, to_left(): return lax.ppermute(a, 'ctx', move(-4))  10.8 us
    ppermute x6, starting transfers between devices, to_left(): return lax.ppermute(a, 'ctx', move(-4))  9.6 us
    ppermute x6, waiting for transfers between devices, to_right(): return lax.ppermute(a, 'ctx', move(4))  9.58 us
    ppermute x2, waiting for transfers between devices, to_side(): return lax.ppermute(a, 'ctx', swap(2))  9.03 us
    ppermute x4, starting transfers between devices, on_device(): count = count + lax.ppermute(count, 'dp', swap(bit))  7.43 us
  transfers between devices with their start and end apart: 25, of which 8 were waited for; matrix products, arithmetic and copies ran while one was open for 13% of the time, Pallas kernels for 0%

profile of v2, /device:TPU:1, one launch (start us, length us, event | category | flops | bytes accessed | tf_op | source)
XLA Modules:
  0.0 115.1 jit_solution(12658382159037586204)
XLA Ops:
  0.6 3.3 %collective-permute-start = (s32[128]{0:T(128)}, s32[128]{0:T(128)S(1)}, u32[]{:S(2)}, u32[]{:S(2)}) collective-permute-start(s32[128]{0:T(128)} %bitcast.66), channel_id=1, source_target_pairs={{0,1},{1,0},{2,3},{3,2},{4,5},{5,4},{6,7},{7,6},{8,9},{9,8},{10,11... | collective-permute-start | bytes 1544 | tf_op jit(solution)/shard_map/ppermute | solution.py:287
  4.0 1.0 dynamic-slice_bitcast_fusion.6
  5.2 1.3 %slice_bitcast_fusion.1 = (s32[64]{0:T(128)}, s32[64]{0:T(128)}) fusion(s32[1,128]{1,0:T(1,128)} %param.10), kind=kLoop, calls=%fused_computation.49 | loop fusion | bytes 1024 | tf_op jit(solution)/shard_map/slice | solution.py:344
  8.0 1.3 %add_reduce_fusion = s32[]{:T(128)} fusion(s32[128]{0:T(128)S(1)} %collective-permute-done, s32[1,128]{1,0:T(1,128)} %param.10), kind=kLoop, calls=%fused_computation.54 | loop fusion | flops 255 | bytes 1028 | tf_op jit(solution)/shard_map/reduce_sum | solution.py:324
  10.0 1.0 convert_reduce_fusion
  11.1 1.4 %collective-permute-done.1 = f32[8,128]{1,0:T(8,128)S(1)} collective-permute-done((f32[8,128]{1,0:T(8,128)S(1)}, f32[8,128]{1,0:T(8,128)S(1)}, u32[]{:S(2)}, u32[]{:S(2)}) %collective-permute-start.1) | collective-permute-done | bytes 4128 | tf_op jit(solution)/shard_map/ppermute | solution.py:326
  12.5 1.6 %collective-permute-start.2 = (f32[8,128]{1,0:T(8,128)S(1)}, f32[8,128]{1,0:T(8,128)S(1)}, u32[]{:S(2)}, u32[]{:S(2)}) collective-permute-start(f32[8,128]{1,0:T(8,128)S(1)} %broadcast_add_fusion), channel_id=1, source_target_pairs={{0,32},{16,48},{32,0},{48,16},{64,96},{80,112},{96,64},{112,80},{1... | collective-permute-start | bytes 12296 | tf_op jit(solution)/shard_map/ppermute | solution.py:326
  14.2 3.0 %collective-permute-start.4 = (bf16[256,512]{1,0:T(8,128)(2,1)S(1)}, bf16[256,512]{1,0:T(8,128)(2,1)S(1)}, u32[]{:S(2)}, u32[]{:S(2)}) collective-permute-start(bf16[256,512]{1,0:T(8,128)(2,1)S(1)} %pad_maximum_fusion.refs_0_), channel_id=1, source_target_pairs={{0,2},{1,3},{2,0},{3,1},{4,6},{5,7},{6,4},{7,5},{8,10},{9,11},{10,... | collective-permute-start | bytes 786440 | tf_op jit(solution)/shard_map/ppermute | solution.py:284
  17.9 1.3 %collective-permute-start.11 = (bf16[256,512]{1,0:T(8,128)(2,1)S(1)}, bf16[256,512]{1,0:T(8,128)(2,1)S(1)}, u32[]{:S(2)}, u32[]{:S(2)}) collective-permute-start(bf16[256,512]{1,0:T(8,128)(2,1)S(1)} %pad_maximum_fusion.refs_0_), channel_id=1, source_target_pairs={{0,4},{1,5},{2,6},{3,7},{4,8},{5,9},{6,10},{7,11},{8,12},{9,13},{1... | collective-permute-start | bytes 786440 | tf_op jit(solution)/shard_map/ppermute | solution.py:278
  19.2 1.5 %collective-permute-start.9 = (bf16[256,512]{1,0:T(8,128)(2,1)S(1)}, bf16[256,512]{1,0:T(8,128)(2,1)S(1)}, u32[]{:S(2)}, u32[]{:S(2)}) collective-permute-start(bf16[256,512]{1,0:T(8,128)(2,1)S(1)} %pad_maximum_fusion.refs_0_), channel_id=1, source_target_pairs={{0,12},{1,13},{2,14},{3,15},{4,0},{5,1},{6,2},{7,3},{8,4},{9,5},{1... | collective-permute-start | bytes 786440 | tf_op jit(solution)/shard_map/ppermute | solution.py:281
  20.6 1.4 %collective-permute-done.4.refs_1_ = bf16[256,512]{1,0:T(8,128)(2,1)S(1)} collective-permute-done((bf16[256,512]{1,0:T(8,128)(2,1)S(1)}, bf16[256,512]{1,0:T(8,128)(2,1)S(1)}, u32[]{:S(2)}, u32[]{:S(2)}) %collective-permute-start.4) | collective-permute-done | bytes 262176 | tf_op jit(solution)/shard_map/ppermute | solution.py:284
  22.0 4.5 %collective-permute-start.5 = (f32[8,128]{1,0:T(8,128)S(1)}, f32[8,128]{1,0:T(8,128)S(1)}, u32[]{:S(2)}, u32[]{:S(2)}) collective-permute-start(f32[8,128]{1,0:T(8,128)S(1)} %fusion.7), channel_id=1, source_target_pairs={{0,64},{16,80},{32,96},{48,112},{64,0},{80,16},{96,32},{112,48},{1... | collective-permute-start | bytes 12296 | tf_op jit(solution)/shard_map/ppermute | solution.py:329
  27.4 3.2 %collective-permute-start.7 = (bf16[128,2048]{1,0:T(8,128)(2,1)}, bf16[128,2048]{1,0:T(8,128)(2,1)S(1)}, u32[]{:S(2)}, u32[]{:S(2)}) collective-permute-start(bf16[128,2048]{1,0:T(8,128)(2,1)} %get-tuple-element.48), channel_id=1, source_target_pairs={{0,1},{1,0},{2,3},{3,2},{4,5},{5,4},{6,7},{7,6},{8,9},{9,8},{10,11... | collective-permute-start | bytes 1572872 | tf_op jit(solution)/shard_map/ppermute | solution.py:287
  30.5 2.5 %collective-permute-start.10 = (bf16[256,512]{1,0:T(8,128)(2,1)S(1)}, bf16[256,512]{1,0:T(8,128)(2,1)S(1)}, u32[]{:S(2)}, u32[]{:S(2)}) collective-permute-start(bf16[256,512]{1,0:T(8,128)(2,1)S(1)} %collective-permute-done.4.refs_1_), channel_id=1, source_target_pairs={{0,12},{1,13},{2,14},{3,15},{4,0},{5,1},{6,2},{7,3},{8,4},{9,5},{1... | collective-permute-start | bytes 786440 | tf_op jit(solution)/shard_map/ppermute | solution.py:281
  34.3 1.3 %collective-permute-start.6 = (f32[8,128]{1,0:T(8,128)S(1)}, f32[8,128]{1,0:T(8,128)S(1)}, u32[]{:S(2)}, u32[]{:S(2)}) collective-permute-start(f32[8,128]{1,0:T(8,128)S(1)} %add.188), channel_id=1, source_target_pairs={{0,128},{16,144},{32,160},{48,176},{64,192},{80,208},{96,224},{112... | collective-permute-start | bytes 12296 | tf_op jit(solution)/shard_map/ppermute | solution.py:329
  35.6 1.8 %and_select_fusion = s32[2]{0:T(128)} fusion(s32[1]{0:T(128)} %bitcast.8, s32[1]{0:T(128)} %bitcast.7, s32[1]{0:T(128)} %bitcast.1, s32[1]{0:T(128)} %bitcast), kind=kLoop, calls=%fused_computation.35 | loop fusion | flops 38 | bytes 24 | tf_op jit(solution)/shard_map/jit(floor_divide)/jit(_where)/select_n | solution.py:348
  37.6 1.1 collective-permute-done.10.refs_3_
  38.7 3.4 %collective-permute-start.14 = (bf16[256,512]{1,0:T(8,128)(2,1)S(1)}, bf16[256,512]{1,0:T(8,128)(2,1)}, u32[]{:S(2)}, u32[]{:S(2)}) collective-permute-start(bf16[256,512]{1,0:T(8,128)(2,1)S(1)} %collective-permute-done.10.refs_3_), channel_id=1, source_target_pairs={{0,12},{1,13},{2,14},{3,15},{4,0},{5,1},{6,2},{7,3},{8,4},{9,5},{1... | collective-permute-start | bytes 786440 | tf_op jit(solution)/shard_map/ppermute | solution.py:281
  44.3 7.5 %collective-permute-done.13.refs_6_ = bf16[256,512]{1,0:T(8,128)(2,1)} collective-permute-done((bf16[256,512]{1,0:T(8,128)(2,1)S(1)}, bf16[256,512]{1,0:T(8,128)(2,1)}, u32[]{:S(2)}, u32[]{:S(2)}) %collective-permute-start.13) | collective-permute-done | bytes 262176 | tf_op jit(solution)/shard_map/ppermute | solution.py:278
  51.8 17.9 %shard_map.93 = (bf16[128,2048]{1,0:T(8,128)(2,1)S(1)}, bf16[128,2048]{1,0:T(8,128)(2,1)S(1)}, bf16[128,2048]{1,0:T(8,128)(2,1)S(1)}, bf16[128,2048]{1,0:T(8,128...) custom-call(s32[15]{0:T(128)S(1)} %concatenate.49.info_ref, ...), custom_call_target="tpu_custom_call" | custom-call | flops 6000000000 | bytes 8000000 | tf_op jit(solution)/shard_map/pallas_call | solution.py:207
  69.7 9.9 %collective-permute-start.18 = (bf16[528,256]{1,0:T(8,128)(2,1)S(1)}, bf16[528,256]{1,0:T(8,128)(2,1)S(1)}, u32[]{:S(2)}, u32[]{:S(2)}) collective-permute-start(bf16[528,256]{1,0:T(8,128)(2,1)S(1)} %get-tuple-element.32), channel_id=1, source_target_pairs={{0,4},{1,5},{2,6},{3,7},{4,8},{5,9},{6,10},{7,11},{8,12},{9,13},{1... | collective-permute-start | bytes 811016 | tf_op jit(solution)/shard_map/ppermute | solution.py:278
  79.6 1.2 %collective-permute-start.15 = (bf16[128,2048]{1,0:T(8,128)(2,1)S(1)}, bf16[128,2048]{1,0:T(8,128)(2,1)S(1)}, u32[]{:S(2)}, u32[]{:S(2)}) collective-permute-start(bf16[128,2048]{1,0:T(8,128)(2,1)S(1)} %get-tuple-element.26), channel_id=1, source_target_pairs={{0,1},{1,0},{2,3},{3,2},{4,5},{5,4},{6,7},{7,6},{8,9},{9,8},{10,11... | collective-permute-start | bytes 1572872 | tf_op jit(solution)/shard_map/ppermute | solution.py:287
  82.3 2.1 %collective-permute-done.18 = bf16[528,256]{1,0:T(8,128)(2,1)S(1)} collective-permute-done((bf16[528,256]{1,0:T(8,128)(2,1)S(1)}, bf16[528,256]{1,0:T(8,128)(2,1)S(1)}, u32[]{:S(2)}, u32[]{:S(2)}) %collective-permute-start.18) | collective-permute-done | bytes 270368 | tf_op jit(solution)/shard_map/ppermute | solution.py:278
  84.4 3.3 %collective-permute-start.16 = (bf16[128,2048]{1,0:T(8,128)(2,1)S(1)}, bf16[128,2048]{1,0:T(8,128)(2,1)S(1)}, u32[]{:S(2)}, u32[]{:S(2)}) collective-permute-start(bf16[128,2048]{1,0:T(8,128)(2,1)S(1)} %get-tuple-element.28), channel_id=1, source_target_pairs={{0,1},{1,0},{2,3},{3,2},{4,5},{5,4},{6,7},{7,6},{8,9},{9,8},{10,11... | collective-permute-start | bytes 1572872 | tf_op jit(solution)/shard_map/ppermute | solution.py:287
  87.8 1.1 collective-permute-done.21
  88.9 1.2 %collective-permute-start.19 = (bf16[528,256]{1,0:T(8,128)(2,1)S(1)}, bf16[528,256]{1,0:T(8,128)(2,1)S(1)}, u32[]{:S(2)}, u32[]{:S(2)}) collective-permute-start(bf16[528,256]{1,0:T(8,128)(2,1)S(1)} %add_convert_fusion.2), channel_id=1, source_target_pairs={{0,4},{1,5},{2,6},{3,7},{4,8},{5,9},{6,10},{7,11},{8,12},{9,13},{1... | collective-permute-start | bytes 811016 | tf_op jit(solution)/shard_map/ppermute | solution.py:278
  90.2 1.6 %collective-permute-start.22 = (bf16[528,256]{1,0:T(8,128)(2,1)S(1)}, bf16[528,256]{1,0:T(8,128)(2,1)S(1)}, u32[]{:S(2)}, u32[]{:S(2)}) collective-permute-start(bf16[528,256]{1,0:T(8,128)(2,1)S(1)} %add_convert_fusion.1), channel_id=1, source_target_pairs={{0,12},{1,13},{2,14},{3,15},{4,0},{5,1},{6,2},{7,3},{8,4},{9,5},{1... | collective-permute-start | bytes 811016 | tf_op jit(solution)/shard_map/ppermute | solution.py:281
  92.0 8.6 %collective-permute-done.22 = bf16[528,256]{1,0:T(8,128)(2,1)S(1)} collective-permute-done((bf16[528,256]{1,0:T(8,128)(2,1)S(1)}, bf16[528,256]{1,0:T(8,128)(2,1)S(1)}, u32[]{:S(2)}, u32[]{:S(2)}) %collective-permute-start.22) | collective-permute-done | bytes 270368 | tf_op jit(solution)/shard_map/ppermute | solution.py:281
  100.7 1.1 maximum_bitcast_fusion
  101.8 7.6 %collective-permute-done.23.refs_3_ = bf16[528,256]{1,0:T(8,128)(2,1)S(1)} collective-permute-done((bf16[528,256]{1,0:T(8,128)(2,1)S(1)}, bf16[528,256]{1,0:T(8,128)(2,1)S(1)}, u32[]{:S(2)}, u32[]{:S(2)}) %collective-permute-start.23) | collective-permute-done | bytes 270368 | tf_op jit(solution)/shard_map/ppermute | solution.py:284
  110.2 1.7 %collective-permute-start.24 = (bf16[128,512]{1,0:T(8,128)(2,1)S(1)}, bf16[128,512]{1,0:T(8,128)(2,1)S(1)}, u32[]{:S(2)}, u32[]{:S(2)}) collective-permute-start(bf16[128,512]{1,0:T(8,128)(2,1)S(1)} %get-tuple-element.39), channel_id=1, source_target_pairs={{0,1},{1,0},{2,3},{3,2},{4,5},{5,4},{6,7},{7,6},{8,9},{9,8},{10,11... | collective-permute-start | bytes 393224 | tf_op jit(solution)/shard_map/ppermute | solution.py:287
  111.9 1.8 %multiply_convert_fusion = bf16[1,128,4096]{2,1,0:T(8,128)(2,1)} fusion(bf16[1,128,2048]{2,1,0:T(8,128)(2,1)S(1)} %get-tuple-element.43, bf16[1,128,2048]{2,1,0:T(8,128)(2,1)S(1)} %get-tuple-element.42, f32[]{:T(128)} %bitcast.39), kind=kLoop, calls=%fused_computation | loop fusion | flops 3145728 | bytes 2097156 | tf_op jit(solution)/shard_map/convert_element_type | solution.py:387
  (74 shorter events, 10.4 us)
Async XLA Ops:
  0.6 7.4 %collective-permute-start = (s32[128]{0:T(128)}, s32[128]{0:T(128)S(1)}, u32[]{:S(2)}, u32[]{:S(2)}) collective-permute-start(s32[128]{0:T(128)} %bitcast.66), channel_id=1, source_target_pairs={{0,1},{1,0},{2,3},{3,2},{4,5},{5,4},{6,7},{7,6},{8,9},{9,8},{10,11... | collective-permute-start | bytes 1544 | tf_op jit(solution)/shard_map/ppermute | solution.py:287
  4.0 22.5 %copy-start = (bf16[1,128,4096]{2,1,0:T(8,128)(2,1)S(1)}, bf16[1,128,4096]{2,1,0:T(8,128)(2,1)}, u32[]{:S(2)}) copy-start(bf16[1,128,4096]{2,1,0:T(8,128)(2,1)} %param.6) | copy-start | bytes 3145732
  5.0 9.1 %collective-permute-start.3 = (bf16[128,512]{1,0:T(8,128)(2,1)S(1)}, bf16[128,512]{1,0:T(8,128)(2,1)S(1)}, u32[]{:S(2)}, u32[]{:S(2)}) collective-permute-start(bf16[128,512]{1,0:T(8,128)(2,1)S(1)} %pad_maximum_fusion.2), channel_id=1, source_target_pairs={{0,1},{1,0},{2,3},{3,2},{4,5},{5,4},{6,7},{7,6},{8,9},{9,8},{10,11... | collective-permute-start | bytes 393224 | tf_op jit(solution)/shard_map/ppermute | solution.py:287
  8.0 14.0 %copy-start.3 = (s32[128]{0:T(128)}, s32[128]{0:T(128)S(1)}, u32[]{:S(2)}) copy-start(s32[128]{0:T(128)S(1)} %collective-permute-done) | copy-start | bytes 1540
  9.9 2.5 %collective-permute-start.1 = (f32[8,128]{1,0:T(8,128)S(1)}, f32[8,128]{1,0:T(8,128)S(1)}, u32[]{:S(2)}, u32[]{:S(2)}) collective-permute-start(f32[8,128]{1,0:T(8,128)S(1)} %broadcast_in_dim.14), channel_id=1, source_target_pairs={{0,16},{16,0},{32,48},{48,32},{64,80},{80,64},{96,112},{112,96},{1... | collective-permute-start | bytes 12296 | tf_op jit(solution)/shard_map/ppermute | solution.py:326
  12.5 5.4 %collective-permute-start.2 = (f32[8,128]{1,0:T(8,128)S(1)}, f32[8,128]{1,0:T(8,128)S(1)}, u32[]{:S(2)}, u32[]{:S(2)}) collective-permute-start(f32[8,128]{1,0:T(8,128)S(1)} %broadcast_add_fusion), channel_id=1, source_target_pairs={{0,32},{16,48},{32,0},{48,16},{64,96},{80,112},{96,64},{112,80},{1... | collective-permute-start | bytes 12296 | tf_op jit(solution)/shard_map/ppermute | solution.py:326
  14.2 7.8 %collective-permute-start.4 = (bf16[256,512]{1,0:T(8,128)(2,1)S(1)}, bf16[256,512]{1,0:T(8,128)(2,1)S(1)}, u32[]{:S(2)}, u32[]{:S(2)}) collective-permute-start(bf16[256,512]{1,0:T(8,128)(2,1)S(1)} %pad_maximum_fusion.refs_0_), channel_id=1, source_target_pairs={{0,2},{1,3},{2,0},{3,1},{4,6},{5,7},{6,4},{7,5},{8,10},{9,11},{10,... | collective-permute-start | bytes 786440 | tf_op jit(solution)/shard_map/ppermute | solution.py:284
  17.9 15.2 %copy-start.1 = (bf16[1,128,4096]{2,1,0:T(8,128)(2,1)S(1)}, bf16[1,128,4096]{2,1,0:T(8,128)(2,1)}, u32[]{:S(2)}) copy-start(bf16[1,128,4096]{2,1,0:T(8,128)(2,1)} %param.9) | copy-start | bytes 3145732
  17.9 16.4 %collective-permute-start.11 = (bf16[256,512]{1,0:T(8,128)(2,1)S(1)}, bf16[256,512]{1,0:T(8,128)(2,1)S(1)}, u32[]{:S(2)}, u32[]{:S(2)}) collective-permute-start(bf16[256,512]{1,0:T(8,128)(2,1)S(1)} %pad_maximum_fusion.refs_0_), channel_id=1, source_target_pairs={{0,4},{1,5},{2,6},{3,7},{4,8},{5,9},{6,10},{7,11},{8,12},{9,13},{1... | collective-permute-start | bytes 786440 | tf_op jit(solution)/shard_map/ppermute | solution.py:278
  19.2 18.2 %collective-permute-start.9 = (bf16[256,512]{1,0:T(8,128)(2,1)S(1)}, bf16[256,512]{1,0:T(8,128)(2,1)S(1)}, u32[]{:S(2)}, u32[]{:S(2)}) collective-permute-start(bf16[256,512]{1,0:T(8,128)(2,1)S(1)} %pad_maximum_fusion.refs_0_), channel_id=1, source_target_pairs={{0,12},{1,13},{2,14},{3,15},{4,0},{5,1},{6,2},{7,3},{8,4},{9,5},{1... | collective-permute-start | bytes 786440 | tf_op jit(solution)/shard_map/ppermute | solution.py:281
  22.0 11.9 %collective-permute-start.5 = (f32[8,128]{1,0:T(8,128)S(1)}, f32[8,128]{1,0:T(8,128)S(1)}, u32[]{:S(2)}, u32[]{:S(2)}) collective-permute-start(f32[8,128]{1,0:T(8,128)S(1)} %fusion.7), channel_id=1, source_target_pairs={{0,64},{16,80},{32,96},{48,112},{64,0},{80,16},{96,32},{112,48},{1... | collective-permute-start | bytes 12296 | tf_op jit(solution)/shard_map/ppermute | solution.py:329
  27.4 14.7 %copy-start.4 = (s32[128]{0:T(128)S(1)}, s32[128]{0:T(128)}, u32[]{:S(2)}) copy-start(s32[128]{0:T(128)} %copy-done.3) | copy-start | bytes 1540
  27.4 14.8 %copy-start.5 = (s32[64]{0:T(128)S(1)}, s32[64]{0:T(128)}, u32[]{:S(2)}) copy-start(s32[64]{0:T(128)} %get-tuple-element.66) | copy-start | bytes 772
  27.4 14.8 %copy-start.6 = (s32[64]{0:T(128)S(1)}, s32[64]{0:T(128)}, u32[]{:S(2)}) copy-start(s32[64]{0:T(128)} %get-tuple-element.67) | copy-start | bytes 772
  27.4 14.9 %copy-start.2 = (s32[256]{0:T(256)S(1)}, s32[256]{0:T(256)}, u32[]{:S(2)}) copy-start(s32[256]{0:T(256)} %get-tuple-element.71) | copy-start | bytes 3076
  27.4 24.4 %collective-permute-start.7 = (bf16[128,2048]{1,0:T(8,128)(2,1)}, bf16[128,2048]{1,0:T(8,128)(2,1)S(1)}, u32[]{:S(2)}, u32[]{:S(2)}) collective-permute-start(bf16[128,2048]{1,0:T(8,128)(2,1)} %get-tuple-element.48), channel_id=1, source_target_pairs={{0,1},{1,0},{2,3},{3,2},{4,5},{5,4},{6,7},{7,6},{8,9},{9,8},{10,11... | collective-permute-start | bytes 1572872 | tf_op jit(solution)/shard_map/ppermute | solution.py:287
  30.5 8.1 %collective-permute-start.10 = (bf16[256,512]{1,0:T(8,128)(2,1)S(1)}, bf16[256,512]{1,0:T(8,128)(2,1)S(1)}, u32[]{:S(2)}, u32[]{:S(2)}) collective-permute-start(bf16[256,512]{1,0:T(8,128)(2,1)S(1)} %collective-permute-done.4.refs_1_), channel_id=1, source_target_pairs={{0,12},{1,13},{2,14},{3,15},{4,0},{5,1},{6,2},{7,3},{8,4},{9,5},{1... | collective-permute-start | bytes 786440 | tf_op jit(solution)/shard_map/ppermute | solution.py:281
  33.9 17.9 %collective-permute-start.8 = (bf16[128,2048]{1,0:T(8,128)(2,1)}, bf16[128,2048]{1,0:T(8,128)(2,1)S(1)}, u32[]{:S(2)}, u32[]{:S(2)}) collective-permute-start(bf16[128,2048]{1,0:T(8,128)(2,1)} %get-tuple-element.46), channel_id=1, source_target_pairs={{0,1},{1,0},{2,3},{3,2},{4,5},{5,4},{6,7},{7,6},{8,9},{9,8},{10,11... | collective-permute-start | bytes 1572872 | tf_op jit(solution)/shard_map/ppermute | solution.py:287
  34.3 3.1 %collective-permute-start.6 = (f32[8,128]{1,0:T(8,128)S(1)}, f32[8,128]{1,0:T(8,128)S(1)}, u32[]{:S(2)}, u32[]{:S(2)}) collective-permute-start(f32[8,128]{1,0:T(8,128)S(1)} %add.188), channel_id=1, source_target_pairs={{0,128},{16,144},{32,160},{48,176},{64,192},{80,208},{96,224},{112... | collective-permute-start | bytes 12296 | tf_op jit(solution)/shard_map/ppermute | solution.py:329
  37.4 14.4 %collective-permute-start.12 = (bf16[256,512]{1,0:T(8,128)(2,1)S(1)}, bf16[256,512]{1,0:T(8,128)(2,1)}, u32[]{:S(2)}, u32[]{:S(2)}) collective-permute-start(bf16[256,512]{1,0:T(8,128)(2,1)S(1)} %collective-permute-done.4.refs_1_), channel_id=1, source_target_pairs={{0,4},{1,5},{2,6},{3,7},{4,8},{5,9},{6,10},{7,11},{8,12},{9,13},{1... | collective-permute-start | bytes 786440 | tf_op jit(solution)/shard_map/ppermute | solution.py:278
  37.4 14.4 %collective-permute-start.13 = (bf16[256,512]{1,0:T(8,128)(2,1)S(1)}, bf16[256,512]{1,0:T(8,128)(2,1)}, u32[]{:S(2)}, u32[]{:S(2)}) collective-permute-start(bf16[256,512]{1,0:T(8,128)(2,1)S(1)} %collective-permute-done.11.refs_4_), channel_id=1, source_target_pairs={{0,4},{1,5},{2,6},{3,7},{4,8},{5,9},{6,10},{7,11},{8,12},{9,13},{1... | collective-permute-start | bytes 786440 | tf_op jit(solution)/shard_map/ppermute | solution.py:278
  38.7 13.1 %collective-permute-start.14 = (bf16[256,512]{1,0:T(8,128)(2,1)S(1)}, bf16[256,512]{1,0:T(8,128)(2,1)}, u32[]{:S(2)}, u32[]{:S(2)}) collective-permute-start(bf16[256,512]{1,0:T(8,128)(2,1)S(1)} %collective-permute-done.10.refs_3_), channel_id=1, source_target_pairs={{0,12},{1,13},{2,14},{3,15},{4,0},{5,1},{6,2},{7,3},{8,4},{9,5},{1... | collective-permute-start | bytes 786440 | tf_op jit(solution)/shard_map/ppermute | solution.py:281
  69.7 14.7 %collective-permute-start.18 = (bf16[528,256]{1,0:T(8,128)(2,1)S(1)}, bf16[528,256]{1,0:T(8,128)(2,1)S(1)}, u32[]{:S(2)}, u32[]{:S(2)}) collective-permute-start(bf16[528,256]{1,0:T(8,128)(2,1)S(1)} %get-tuple-element.32), channel_id=1, source_target_pairs={{0,4},{1,5},{2,6},{3,7},{4,8},{5,9},{6,10},{7,11},{8,12},{9,13},{1... | collective-permute-start | bytes 811016 | tf_op jit(solution)/shard_map/ppermute | solution.py:278
  79.6 10.6 %collective-permute-start.15 = (bf16[128,2048]{1,0:T(8,128)(2,1)S(1)}, bf16[128,2048]{1,0:T(8,128)(2,1)S(1)}, u32[]{:S(2)}, u32[]{:S(2)}) collective-permute-start(bf16[128,2048]{1,0:T(8,128)(2,1)S(1)} %get-tuple-element.26), channel_id=1, source_target_pairs={{0,1},{1,0},{2,3},{3,2},{4,5},{5,4},{6,7},{7,6},{8,9},{9,8},{10,11... | collective-permute-start | bytes 1572872 | tf_op jit(solution)/shard_map/ppermute | solution.py:287
  80.8 8.1 %collective-permute-start.21 = (bf16[528,256]{1,0:T(8,128)(2,1)S(1)}, bf16[528,256]{1,0:T(8,128)(2,1)S(1)}, u32[]{:S(2)}, u32[]{:S(2)}) collective-permute-start(bf16[528,256]{1,0:T(8,128)(2,1)S(1)} %get-tuple-element.36), channel_id=1, source_target_pairs={{0,12},{1,13},{2,14},{3,15},{4,0},{5,1},{6,2},{7,3},{8,4},{9,5},{1... | collective-permute-start | bytes 811016 | tf_op jit(solution)/shard_map/ppermute | solution.py:281
  80.8 21.0 %collective-permute-start.17 = (bf16[528,256]{1,0:T(8,128)(2,1)S(1)}, bf16[528,256]{1,0:T(8,128)(2,1)S(1)}, u32[]{:S(2)}, u32[]{:S(2)}) collective-permute-start(bf16[528,256]{1,0:T(8,128)(2,1)S(1)} %get-tuple-element.30), channel_id=1, source_target_pairs={{0,12},{1,13},{2,14},{3,15},{4,0},{5,1},{6,2},{7,3},{8,4},{9,5},{1... | collective-permute-start | bytes 811016 | tf_op jit(solution)/shard_map/ppermute | solution.py:281
  81.5 10.5 %collective-permute-start.20 = (bf16[528,256]{1,0:T(8,128)(2,1)S(1)}, bf16[528,256]{1,0:T(8,128)(2,1)S(1)}, u32[]{:S(2)}, u32[]{:S(2)}) collective-permute-start(bf16[528,256]{1,0:T(8,128)(2,1)S(1)} %get-tuple-element.34), channel_id=1, source_target_pairs={{0,4},{1,5},{2,6},{3,7},{4,8},{5,9},{6,10},{7,11},{8,12},{9,13},{1... | collective-permute-start | bytes 811016 | tf_op jit(solution)/shard_map/ppermute | solution.py:278
  84.4 7.4 %collective-permute-start.16 = (bf16[128,2048]{1,0:T(8,128)(2,1)S(1)}, bf16[128,2048]{1,0:T(8,128)(2,1)S(1)}, u32[]{:S(2)}, u32[]{:S(2)}) collective-permute-start(bf16[128,2048]{1,0:T(8,128)(2,1)S(1)} %get-tuple-element.28), channel_id=1, source_target_pairs={{0,1},{1,0},{2,3},{3,2},{4,5},{5,4},{6,7},{7,6},{8,9},{9,8},{10,11... | collective-permute-start | bytes 1572872 | tf_op jit(solution)/shard_map/ppermute | solution.py:287
  88.9 12.9 %collective-permute-start.19 = (bf16[528,256]{1,0:T(8,128)(2,1)S(1)}, bf16[528,256]{1,0:T(8,128)(2,1)S(1)}, u32[]{:S(2)}, u32[]{:S(2)}) collective-permute-start(bf16[528,256]{1,0:T(8,128)(2,1)S(1)} %add_convert_fusion.2), channel_id=1, source_target_pairs={{0,4},{1,5},{2,6},{3,7},{4,8},{5,9},{6,10},{7,11},{8,12},{9,13},{1... | collective-permute-start | bytes 811016 | tf_op jit(solution)/shard_map/ppermute | solution.py:278
  90.2 10.3 %collective-permute-start.22 = (bf16[528,256]{1,0:T(8,128)(2,1)S(1)}, bf16[528,256]{1,0:T(8,128)(2,1)S(1)}, u32[]{:S(2)}, u32[]{:S(2)}) collective-permute-start(bf16[528,256]{1,0:T(8,128)(2,1)S(1)} %add_convert_fusion.1), channel_id=1, source_target_pairs={{0,12},{1,13},{2,14},{3,15},{4,0},{5,1},{6,2},{7,3},{8,4},{9,5},{1... | collective-permute-start | bytes 811016 | tf_op jit(solution)/shard_map/ppermute | solution.py:281
  100.6 8.8 %collective-permute-start.23 = (bf16[528,256]{1,0:T(8,128)(2,1)S(1)}, bf16[528,256]{1,0:T(8,128)(2,1)S(1)}, u32[]{:S(2)}, u32[]{:S(2)}) collective-permute-start(bf16[528,256]{1,0:T(8,128)(2,1)S(1)} %add_convert_fusion), channel_id=1, source_target_pairs={{0,2},{1,3},{2,0},{3,1},{4,6},{5,7},{6,4},{7,5},{8,10},{9,11},{10,... | collective-permute-start | bytes 811016 | tf_op jit(solution)/shard_map/ppermute | solution.py:284
  110.2 3.5 %collective-permute-start.24 = (bf16[128,512]{1,0:T(8,128)(2,1)S(1)}, bf16[128,512]{1,0:T(8,128)(2,1)S(1)}, u32[]{:S(2)}, u32[]{:S(2)}) collective-permute-start(bf16[128,512]{1,0:T(8,128)(2,1)S(1)} %get-tuple-element.39), channel_id=1, source_target_pairs={{0,1},{1,0},{2,3},{3,2},{4,5},{5,4},{6,7},{7,6},{8,9},{9,8},{10,11... | collective-permute-start | bytes 393224 | tf_op jit(solution)/shard_map/ppermute | solution.py:287
